TPU v7x, 128 devices: a whole 4x4x4 slice. The times are simulated.
128 devices in a mesh: gx: 8 (over z, core), gy: 16 (over y, x).
Axes of the slice: x: 4, y: 4, z: 4, core: 2. Of those that a mesh axis runs over, the one named last changes fastest.
Arguments:
- features: bfloat16 [8, 16, 4, 512, 128], P('gx', 'gy'), may hold values from -6 to 6
- slot_cell: int32 [8, 16, 4], P('gx', 'gy'), may hold values from -1 to 7, as said below
- neighbours: int32 [8, 16, 4, 26], P('gx', 'gy'), may hold values from -1 to 35, as said below
- first_weight: bfloat16 [3, 3, 3, 128, 128], replicated, may hold values from -0.109375 to 0.109375
- first_bias: float32 [128], replicated, may hold values from -3 to 3
- second_weight: bfloat16 [3, 3, 3, 128, 128], replicated, may hold values from -0.109375 to 0.109375
- second_bias: float32 [128], replicated, may hold values from -3 to 3
- coarse_weight: bfloat16 [3, 3, 3, 128, 256], replicated, may hold values from -0.109375 to 0.109375
- coarse_bias: float32 [256], replicated, may hold values from -3 to 3
- lift_weight: bfloat16 [256, 128], replicated, may hold values from -0.375 to 0.375
Outputs:
- output: float32 [8, 16, 4, 512, 128], P('gx', 'gy')
Inputs may be any that keep to these rules, and one draw needn't show every extreme that they name: `slot_cell`: in every tile the live slots are slots 0 to n - 1, with n from 1 to 4, and name distinct cells of the tile's 2 x 2 x 2 cells; the other slots hold -1; some tile holds 4 live bricks in every draw, and some tile only one. `neighbours`: the entries agree with slot_cell: entry k of a live slot names the live brick at that brick offset, which lies in the tile itself or one of its 8 neighbour tiles, and is -1 where that cell is empty or outside the scene; all entries of empty slots are -1.
All inputs are finite; a program needn't handle non-finite values.
Results may differ from a plain program's by a relative error of at most 0.0022.
Values may be sent and summed in bfloat16 or wider, within the bound.
A program may use at most 128 MiB of HBM per device.

v0:
```python
import functools

import jax
import jax.numpy as jnp
from jax import lax
from jax.experimental import pallas as pl
from jax.experimental.pallas import tpu as pltpu
from jax.sharding import PartitionSpec as P

MESH = pl.DeviceIdType.MESH
F32 = jnp.float32
BF16 = jnp.bfloat16

OFFSETS = [
    (ox, oy, oz)
    for ox in (-1, 0, 1)
    for oy in (-1, 0, 1)
    for oz in (-1, 0, 1)
    if (ox, oy, oz) != (0, 0, 0)
]
NUMBER = {offset: k for k, offset in enumerate(OFFSETS)}
SIDES = [(-1, 0), (1, 0), (0, -1), (0, 1)]
EDGES = [(-1, -1), (-1, 1), (1, -1), (1, 1)]
ALL = SIDES + EDGES


def edge_of(step, last):
    return last if step < 0 else 0


def kernel(
    gx,
    gy,
    cell,
    nbr,
    feat,
    w1,
    b1,
    w2,
    b2,
    wc,
    bc,
    wl,
    out,
    staged,
    field,
    hidden,
    coarse_field,
    side_src,
    edge_src,
    cside_src,
    cedge_src,
    zin,
    zhid,
    zc,
    w1p,
    w2p,
    wcv,
    wlv,
    joined,
    send_side,
    send_edge,
    recv_side,
    recv_edge,
    csend_side,
    csend_edge,
    crecv_side,
    crecv_edge,
    local_sem,
    out_sem,
    send_sem,
    recv_sem,
):
    mx = lax.axis_index("gx")
    my = lax.axis_index("gy")

    copies = [
        pltpu.make_async_copy(feat, staged, local_sem.at[0]),
        pltpu.make_async_copy(w1, w1p.at[0:3, :, :, 0:128], local_sem.at[1]),
        pltpu.make_async_copy(w1, w1p.at[1:4, :, :, 128:256], local_sem.at[2]),
        pltpu.make_async_copy(w2, w2p.at[0:3, :, :, 0:128], local_sem.at[3]),
        pltpu.make_async_copy(w2, w2p.at[1:4, :, :, 128:256], local_sem.at[4]),
        pltpu.make_async_copy(wc, wcv, local_sem.at[5]),
        pltpu.make_async_copy(wl, wlv, local_sem.at[6]),
    ]
    for copy in copies:
        copy.start()

    def device_at(ox, oy):
        return (lax.rem(mx + ox + gx, gx), lax.rem(my + oy + gy, gy))

    barrier = pltpu.get_barrier_semaphore()
    for ox, oy in ALL:
        pl.semaphore_signal(
            barrier, inc=1, device_id=device_at(ox, oy), device_id_type=MESH
        )

    for wp in (w1p, w2p):
        wp[3, :, :, 0:128] = jnp.zeros((3, 384, 128), BF16)
        wp[0, :, :, 128:256] = jnp.zeros((3, 384, 128), BF16)
    field[4] = jnp.zeros((8, 8, 8, 128), F32)
    hidden[4] = jnp.zeros((8, 8, 8, 128), F32)
    coarse_field[4] = jnp.zeros((4, 4, 8, 128), F32)
    for d in range(4):
        side_src[d, 8] = jnp.zeros((8, 8, 128), F32)
        cside_src[d, 8] = jnp.zeros((4, 8, 128), F32)
        edge_src[d, 16] = jnp.zeros((1, 8, 128), F32)
        cedge_src[d, 16] = jnp.zeros((1, 8, 128), F32)

    live = [jnp.where(cell[s] >= 0, 1.0, 0.0).astype(F32) for s in range(4)]

    def index(s, ox, oy, oz):
        if (ox, oy, oz) == (0, 0, 0):
            return s
        entry = nbr[s, NUMBER[ox, oy, oz]]
        safe = jnp.maximum(entry, 0)
        block = lax.shift_right_logical(safe, 2)
        slot = lax.bitwise_and(safe, 3)
        if (ox, oy) == (0, 0):
            return jnp.where(entry < 0, 4, slot)
        if ox == 0 or oy == 0:
            place = slot + jnp.where(block == 4, 0, 4)
            return jnp.where(entry < 0, 8, place)
        beside_x = (ox + 1) * 3 + 1
        beside_y = 3 + (oy + 1)
        place = slot + jnp.where(
            block == 4,
            0,
            jnp.where(block == beside_x, 4, jnp.where(block == beside_y, 8, 12)),
        )
        return jnp.where(entry < 0, 16, place)

    where = {
        (s, ox, oy, oz): index(s, ox, oy, oz)
        for s in range(4)
        for ox in (-1, 0, 1)
        for oy in (-1, 0, 1)
        for oz in (-1, 0, 1)
    }

    def shifted(low, own, high, step):
        row = lax.broadcasted_iota(jnp.int32, own.shape, own.ndim - 2)
        axis = own.ndim - 2
        down = pltpu.roll(jnp.where(row >= 8 - step, low, own), step, axis)
        up = pltpu.roll(jnp.where(row < step, high, own), 8 - step, axis)
        return down, own, up

    def pair(fetch, ox, oy, step):
        for half in (0, 1):
            parts = [
                shifted(
                    *[fetch(where[s, ox, oy, oz]) for oz in (-1, 0, 1)], step
                )
                for s in (2 * half, 2 * half + 1)
            ]
            for kz in range(3):
                both = jnp.concatenate([parts[0][kz], parts[1][kz]], axis=-2)
                yield slice(16 * half, 16 * half + 16), slice(
                    128 * kz, 128 * kz + 128
                ), both.astype(BF16)

    def fine_centre(source, z):
        def body(m, carry):
            for parity in (0, 1):
                x = 2 * m + parity
                for rows, lanes, value in pair(lambda q: source[q, x], 0, 0, 1):
                    if parity == 0:
                        z[1, m, 1:9, rows, lanes] = value
                    else:
                        z[0, m + 1, 1:9, rows, lanes] = value
            return carry

        lax.fori_loop(0, 4, body, 0)

    def fine_rim(z):
        for d, (ox, oy) in enumerate(SIDES):
            for rows, lanes, value in pair(lambda q: side_src[d, q], ox, oy, 1):
                if ox < 0:
                    z[0, 0, 1:9, rows, lanes] = value
                elif ox > 0:
                    z[1, 4, 1:9, rows, lanes] = value
                else:
                    y = 0 if oy < 0 else 9
                    split = value.reshape(4, 2, 16, 128)
                    z[1, 0:4, y, rows, lanes] = split[:, 0]
                    z[0, 1:5, y, rows, lanes] = split[:, 1]
        for d, (ox, oy) in enumerate(EDGES):
            for rows, lanes, value in pair(lambda q: edge_src[d, q], ox, oy, 1):
                y = 0 if oy < 0 else 9
                if ox < 0:
                    z[0, 0, y, rows, lanes] = value[0]
                else:
                    z[1, 4, y, rows, lanes] = value[0]

    def exchange(number, source, last, sides, edges, rsides, redges):
        rows = 8 * (last + 1)
        for d, (ox, oy) in enumerate(SIDES):
            for s in range(4):
                if oy == 0:
                    face = source[s, edge_of(ox, last)]
                else:
                    face = source[s, :, edge_of(oy, last)]
                sides[d, s] = face.reshape(rows, 128).astype(BF16)
        for d, (ox, oy) in enumerate(EDGES):
            edges[d] = jnp.concatenate(
                [source[s, edge_of(ox, last), edge_of(oy, last)] for s in range(4)],
                axis=0,
            ).astype(BF16)
        started = []
        for k, (ox, oy) in enumerate(ALL):
            if k < 4:
                src, dst = sides.at[k], rsides.at[k]
            else:
                src, dst = edges.at[k - 4], redges.at[k - 4]
            started.append(
                pltpu.make_async_remote_copy(
                    src_ref=src,
                    dst_ref=dst,
                    send_sem=send_sem.at[number, k],
                    recv_sem=recv_sem.at[number, k],
                    device_id=device_at(-ox, -oy),
                    device_id_type=MESH,
                )
            )
        return started

    def own_sources(source, last, sides, edges):
        for d, (ox, oy) in enumerate(SIDES):
            for s in range(4):
                if oy == 0:
                    sides[d, s] = source[s, edge_of(ox, last)]
                else:
                    sides[d, s] = source[s, :, edge_of(oy, last)]
        for d, (ox, oy) in enumerate(EDGES):
            for s in range(4):
                edges[d, s, 0] = source[s, edge_of(ox, last), edge_of(oy, last)]

    def received_sources(last, sides, edges, rsides, redges):
        for d in range(4):
            for s in range(4):
                sides[d, 4 + s] = rsides[d, s].astype(F32).reshape(last + 1, 8, 128)
        for d, (ox, oy) in enumerate(EDGES):
            dx = SIDES.index((ox, 0))
            dy = SIDES.index((0, oy))
            column = redges[d].astype(F32)
            for s in range(4):
                edges[d, 4 + s, 0] = sides[dx, 4 + s, edge_of(oy, last)]
                edges[d, 8 + s, 0] = sides[dy, 4 + s, edge_of(ox, last)]
                edges[d, 12 + s, 0] = column[8 * s : 8 * s + 8]

    def fine_pair(z, wp, i):
        lhs = jnp.concatenate(
            [
                z[p % 2, i + p // 2, ky : ky + 8].reshape(256, 384)
                for ky in range(3)
                for p in range(4)
            ],
            axis=1,
        )
        rhs = jnp.concatenate(
            [wp[p, ky] for ky in range(3) for p in range(4)], axis=0
        )
        return jnp.dot(lhs, rhs, preferred_element_type=F32)

    copies[0].wait()
    for s in range(4):
        for x in range(8):
            field[s, x] = staged[s, x].astype(F32).reshape(8, 8, 128)
    sent = exchange(0, field, 7, send_side.at[0], send_edge.at[0], recv_side.at[0], recv_edge.at[0])
    pl.semaphore_wait(barrier, 8)
    for copy in sent:
        copy.start()
    own_sources(field, 7, side_src, edge_src)
    fine_centre(field, zin)
    for copy in sent:
        copy.wait_recv()
    received_sources(7, side_src, edge_src, recv_side.at[0], recv_edge.at[0])
    fine_rim(zin)
    copies[1].wait()
    copies[2].wait()

    bias1 = b1[...].reshape(1, 1, 128)

    def first(i, carry):
        acc = fine_pair(zin, w1p, i)
        for h in (0, 1):
            part = acc[:, 128 * h : 128 * h + 128].reshape(8, 4, 8, 128)
            for s in range(4):
                value = jnp.maximum(part[:, s] + bias1, 0.0) * live[s]
                hidden[s, 2 * i + h] = value.astype(BF16).astype(F32)
        return carry

    lax.fori_loop(0, 4, first, 0)
    sent_hidden = exchange(1, hidden, 7, send_side.at[1], send_edge.at[1], recv_side.at[1], recv_edge.at[1])
    for copy in sent_hidden:
        copy.start()
    own_sources(hidden, 7, side_src, edge_src)
    fine_centre(hidden, zhid)
    for copy in sent_hidden:
        copy.wait_recv()
    received_sources(7, side_src, edge_src, recv_side.at[1], recv_edge.at[1])
    fine_rim(zhid)
    copies[3].wait()
    copies[4].wait()

    bias2 = b2[...].reshape(1, 1, 128)

    def second(i, carry):
        acc = fine_pair(zhid, w2p, i)
        for s in range(4):
            summed = None
            for h in (0, 1):
                part = acc[:, 128 * h : 128 * h + 128].reshape(8, 4, 8, 128)
                value = (part[:, s] + bias2 + field[s, 2 * i + h]) * live[s]
                joined[s, 2 * i + h] = value
                summed = value if summed is None else summed + value
            rows = summed.reshape(4, 2, 8, 128)
            rows = rows[:, 0] + rows[:, 1]
            even = lax.broadcasted_iota(jnp.int32, rows.shape, 1) % 2 == 0
            other = jnp.where(even, pltpu.roll(rows, 7, 1), pltpu.roll(rows, 1, 1))
            mean = (rows + other) * 0.125
            coarse_field[s, i] = mean.astype(BF16).astype(F32)
        return carry

    lax.fori_loop(0, 4, second, 0)
    sent_coarse = exchange(2, coarse_field, 3, csend_side, csend_edge, crecv_side, crecv_edge)
    for copy in sent_coarse:
        copy.start()
    own_sources(coarse_field, 3, cside_src, cedge_src)
    for x in range(4):
        for rows, lanes, value in pair(lambda q: coarse_field[q, x], 0, 0, 2):
            zc[x + 1, 1:5, rows, lanes] = value
    for copy in sent_coarse:
        copy.wait_recv()
    received_sources(3, cside_src, cedge_src, crecv_side, crecv_edge)
    for d, (ox, oy) in enumerate(SIDES):
        for rows, lanes, value in pair(lambda q: cside_src[d, q], ox, oy, 2):
            if oy == 0:
                zc[0 if ox < 0 else 5, 1:5, rows, lanes] = value
            else:
                zc[1:5, 0 if oy < 0 else 5, rows, lanes] = value
    for d, (ox, oy) in enumerate(EDGES):
        for rows, lanes, value in pair(lambda q: cedge_src[d, q], ox, oy, 2):
            zc[0 if ox < 0 else 5, 0 if oy < 0 else 5, rows, lanes] = value[0]

    copies[5].wait()
    copies[6].wait()
    bias = bc[...]

    def last(x, carry):
        lhs = jnp.concatenate(
            [
                zc[x + kx, ky : ky + 4].reshape(128, 384)
                for kx in range(3)
                for ky in range(3)
            ],
            axis=1,
        )
        acc = jnp.dot(lhs, wcv[...], preferred_element_type=F32)
        acc = jnp.maximum(acc + bias, 0.0).reshape(4, 4, 8, 256)
        acc = jnp.concatenate(
            [(acc[:, s] * live[s])[:, None] for s in range(4)], axis=1
        )
        lifted = jnp.dot(
            acc.reshape(128, 256).astype(BF16), wlv[...], preferred_element_type=F32
        ).reshape(4, 1, 4, 8, 128)
        for s in range(4):
            raised = jnp.broadcast_to(lifted[:, :, s], (4, 2, 8, 128)).reshape(8, 8, 128)
            for h in (0, 1):
                joined[s, 2 * x + h] = (joined[s, 2 * x + h] + raised) * live[s]
        return carry

    lax.fori_loop(0, 4, last, 0)
    done = pltpu.make_async_copy(joined, out, out_sem)
    done.start()
    for copy in sent + sent_hidden + sent_coarse:
        copy.wait_send()
    done.wait()


def local(gx, gy, features, slot_cell, neighbours, w1, b1, w2, b2, wc, bc, wl):
    smem = pl.BlockSpec(memory_space=pltpu.SMEM)
    vmem = pl.BlockSpec(memory_space=pltpu.VMEM)
    hbm = pl.BlockSpec(memory_space=pl.ANY)
    result = pl.pallas_call(
        functools.partial(kernel, gx, gy),
        out_shape=jax.ShapeDtypeStruct((4, 8, 8, 8, 128), F32),
        in_specs=[smem, smem, hbm, hbm, vmem, hbm, vmem, hbm, vmem, hbm],
        out_specs=hbm,
        scratch_shapes=[
            pltpu.VMEM((4, 8, 64, 128), BF16),
            pltpu.VMEM((5, 8, 8, 8, 128), F32),
            pltpu.VMEM((5, 8, 8, 8, 128), F32),
            pltpu.VMEM((5, 4, 4, 8, 128), F32),
            pltpu.VMEM((4, 9, 8, 8, 128), F32),
            pltpu.VMEM((4, 17, 1, 8, 128), F32),
            pltpu.VMEM((4, 9, 4, 8, 128), F32),
            pltpu.VMEM((4, 17, 1, 8, 128), F32),
            pltpu.VMEM((2, 5, 10, 32, 384), BF16),
            pltpu.VMEM((2, 5, 10, 32, 384), BF16),
            pltpu.VMEM((6, 6, 32, 384), BF16),
            pltpu.VMEM((4, 3, 384, 256), BF16),
            pltpu.VMEM((4, 3, 384, 256), BF16),
            pltpu.VMEM((3456, 256), BF16),
            pltpu.VMEM((256, 128), BF16),
            pltpu.VMEM((4, 8, 8, 8, 128), F32),
            pltpu.VMEM((2, 4, 4, 64, 128), BF16),
            pltpu.VMEM((2, 4, 32, 128), BF16),
            pltpu.VMEM((2, 4, 4, 64, 128), BF16),
            pltpu.VMEM((2, 4, 32, 128), BF16),
            pltpu.VMEM((4, 4, 32, 128), BF16),
            pltpu.VMEM((4, 32, 128), BF16),
            pltpu.VMEM((4, 4, 32, 128), BF16),
            pltpu.VMEM((4, 32, 128), BF16),
            pltpu.SemaphoreType.DMA((7,)),
            pltpu.SemaphoreType.DMA,
            pltpu.SemaphoreType.DMA((3, 8)),
            pltpu.SemaphoreType.DMA((3, 8)),
        ],
        compiler_params=pltpu.CompilerParams(
            collective_id=0, has_side_effects=True, vmem_limit_bytes=48 * 2**20
        ),
        cost_estimate=pl.CostEstimate(
            flops=8_000_000_000, bytes_accessed=8_000_000, transcendentals=0
        ),
        name="unet_window",
    )(
        slot_cell.reshape(4),
        neighbours.reshape(4, 26),
        features.reshape(4, 8, 64, 128),
        w1.reshape(3, 3, 384, 128),
        b1.reshape(1, 128),
        w2.reshape(3, 3, 384, 128),
        b2.reshape(1, 128),
        wc.reshape(3456, 256),
        bc.reshape(1, 256),
        wl,
    )
    return result.reshape(1, 1, 4, 512, 128)


def solution(mesh):
    placed = (
        P("gx", "gy", None, None, None),
        P("gx", "gy", None),
        P("gx", "gy", None, None),
    ) + (P(),) * 7
    return jax.shard_map(
        functools.partial(local, mesh.shape["gx"], mesh.shape["gy"]),
        mesh=mesh,
        in_specs=placed,
        out_specs=P("gx", "gy", None, None, None),
        check_vma=False,
    )
```

profile of v0, /device:TPU:1, one launch (start us, length us, event | category | flops | bytes accessed | tf_op | source)
XLA Modules:
  0.0 45.6 jit_solution(7134918046943078419)
XLA Ops:
  0.0 0.0 copy-start
  0.0 1.5 %copy-done = bf16[3,3,3,128,256]{4,3,2,1,0:T(8,128)(2,1)S(1)} copy-done((bf16[3,3,3,128,256]{4,3,2,1,0:T(8,128)(2,1)S(1)}, bf16[3,3,3,128,256]{4,3,2,1,0:T(8,128)(2,1)}, u32[]{:S(2)}) %copy-start) | copy-done | bytes 1769496
  1.5 0.0 copy-start.1
  1.5 1.2 %copy-done.1 = bf16[3,3,3,128,128]{4,3,2,1,0:T(8,128)(2,1)S(1)} copy-done((bf16[3,3,3,128,128]{4,3,2,1,0:T(8,128)(2,1)S(1)}, bf16[3,3,3,128,128]{4,3,2,1,0:T(8,128)(2,1)}, u32[]{:S(2)}) %copy-start.1) | copy-done | bytes 884760
  2.6 0.0 copy-start.2
  2.6 1.2 %copy-done.2 = bf16[3,3,3,128,128]{4,3,2,1,0:T(8,128)(2,1)S(1)} copy-done((bf16[3,3,3,128,128]{4,3,2,1,0:T(8,128)(2,1)S(1)}, bf16[3,3,3,128,128]{4,3,2,1,0:T(8,128)(2,1)}, u32[]{:S(2)}) %copy-start.2) | copy-done | bytes 884760
  3.8 0.0 copy-start.3
  3.8 1.0 %copy-done.3 = bf16[1,1,4,512,128]{4,3,2,1,0:T(8,128)(2,1)S(1)} copy-done((bf16[1,1,4,512,128]{4,3,2,1,0:T(8,128)(2,1)S(1)}, bf16[1,1,4,512,128]{4,3,2,1,0:T(8,128)(2,1)}, u32[]{:S(2)}) %copy-start.3) | copy-done | bytes 524312
  4.9 0.0 copy-start.4
  4.9 0.8 %copy-done.4 = bf16[256,128]{1,0:T(8,128)(2,1)S(1)} copy-done((bf16[256,128]{1,0:T(8,128)(2,1)S(1)}, bf16[256,128]{1,0:T(8,128)(2,1)}, u32[]{:S(2)}) %copy-start.4) | copy-done | bytes 65560
  5.7 0.0 copy-start.5
  5.7 0.7 %copy-done.5 = s32[1,1,4,26]{3,2,1,0:T(4,128)S(1)} copy-done((s32[1,1,4,26]{3,2,1,0:T(4,128)S(1)}, s32[1,1,4,26]{3,2,1,0:T(4,128)}, u32[]{:S(2)}) %copy-start.5) | copy-done | bytes 440
  6.4 0.0 copy-start.6
  6.4 0.7 %copy-done.6 = f32[256]{0:T(256)S(1)} copy-done((f32[256]{0:T(256)S(1)}, f32[256]{0:T(256)}, u32[]{:S(2)}) %copy-start.6) | copy-done | bytes 1048
  7.1 0.0 copy-start.7
  7.1 0.7 %copy-done.7 = s32[1,1,4]{2,1,0:T(1,128)S(1)} copy-done((s32[1,1,4]{2,1,0:T(1,128)S(1)}, s32[1,1,4]{2,1,0:T(1,128)}, u32[]{:S(2)}) %copy-start.7) | copy-done | bytes 40
  7.7 0.0 copy-start.8
  7.7 0.7 %copy-done.8 = f32[128]{0:T(128)S(1)} copy-done((f32[128]{0:T(128)S(1)}, f32[128]{0:T(128)}, u32[]{:S(2)}) %copy-start.8) | copy-done | bytes 536
  8.4 0.0 copy-start.9
  8.4 0.7 %copy-done.9 = f32[128]{0:T(128)S(1)} copy-done((f32[128]{0:T(128)S(1)}, f32[128]{0:T(128)}, u32[]{:S(2)}) %copy-start.9) | copy-done | bytes 536
  9.0 35.6 %unet_window.1 = f32[4,8,8,8,128]{4,3,2,1,0:T(8,128)S(1)} custom-call(s32[4]{0:T(128)S(1)} %bitcast.17, s32[4,26]{1,0:T(4,128)S(1)} %bitcast.15, bf16[4,8,64,128]{3,2,1,0:T(8,128)(2,1)S(1)} %bitcast.14, bf16[3,3,384,128]{3,2,1,0:T(8,128)(2,1)S(1)} %bitcast.12, f32[1,128]{1,0:T(1,128)S(1)} %bitcast.18, bf16[3,3,384,128]{3,2,1,0:T(8,128)(2,1)S(1)} %bitcast.13, ...), custom_call_target="tpu_custom_call" | custom-call | flops 8000000000 | bytes 8000000 | tf_op jit(solution)/shard_map/unet_window/pallas_call | solution.py:385
  44.6 1.0 %copy.12 = f32[1,1,4,512,128]{4,3,2,1,0:T(8,128)} copy(f32[1,1,4,512,128]{4,3,2,1,0:T(8,128)S(1)} %bitcast.10) | data formatting | bytes 2097152
Async XLA Ops:
  0.0 1.5 %copy-start = (bf16[3,3,3,128,256]{4,3,2,1,0:T(8,128)(2,1)S(1)}, bf16[3,3,3,128,256]{4,3,2,1,0:T(8,128)(2,1)}, u32[]{:S(2)}) copy-start(bf16[3,3,3,128,256]{4,3,2,1,0:T(8,128)(2,1)} %param.17) | copy-start | bytes 5308420
  1.5 1.2 %copy-start.1 = (bf16[3,3,3,128,128]{4,3,2,1,0:T(8,128)(2,1)S(1)}, bf16[3,3,3,128,128]{4,3,2,1,0:T(8,128)(2,1)}, u32[]{:S(2)}) copy-start(bf16[3,3,3,128,128]{4,3,2,1,0:T(8,128)(2,1)} %param.13) | copy-start | bytes 2654212
  2.6 1.2 %copy-start.2 = (bf16[3,3,3,128,128]{4,3,2,1,0:T(8,128)(2,1)S(1)}, bf16[3,3,3,128,128]{4,3,2,1,0:T(8,128)(2,1)}, u32[]{:S(2)}) copy-start(bf16[3,3,3,128,128]{4,3,2,1,0:T(8,128)(2,1)} %param.15) | copy-start | bytes 2654212
  3.8 1.0 %copy-start.3 = (bf16[1,1,4,512,128]{4,3,2,1,0:T(8,128)(2,1)S(1)}, bf16[1,1,4,512,128]{4,3,2,1,0:T(8,128)(2,1)}, u32[]{:S(2)}) copy-start(bf16[1,1,4,512,128]{4,3,2,1,0:T(8,128)(2,1)} %param.10) | copy-start | bytes 1572868
  4.9 0.8 %copy-start.4 = (bf16[256,128]{1,0:T(8,128)(2,1)S(1)}, bf16[256,128]{1,0:T(8,128)(2,1)}, u32[]{:S(2)}) copy-start(bf16[256,128]{1,0:T(8,128)(2,1)} %wl.1) | copy-start | bytes 196612
  5.7 0.7 %copy-start.5 = (s32[1,1,4,26]{3,2,1,0:T(4,128)S(1)}, s32[1,1,4,26]{3,2,1,0:T(4,128)}, u32[]{:S(2)}) copy-start(s32[1,1,4,26]{3,2,1,0:T(4,128)} %param.12) | copy-start | bytes 1252
  6.4 0.7 %copy-start.6 = (f32[256]{0:T(256)S(1)}, f32[256]{0:T(256)}, u32[]{:S(2)}) copy-start(f32[256]{0:T(256)} %param.18) | copy-start | bytes 3076
  7.1 0.7 %copy-start.7 = (s32[1,1,4]{2,1,0:T(1,128)S(1)}, s32[1,1,4]{2,1,0:T(1,128)}, u32[]{:S(2)}) copy-start(s32[1,1,4]{2,1,0:T(1,128)} %param.11) | copy-start | bytes 52
  7.7 0.7 %copy-start.8 = (f32[128]{0:T(128)S(1)}, f32[128]{0:T(128)}, u32[]{:S(2)}) copy-start(f32[128]{0:T(128)} %param.14) | copy-start | bytes 1540
  8.4 0.7 %copy-start.9 = (f32[128]{0:T(128)S(1)}, f32[128]{0:T(128)}, u32[]{:S(2)}) copy-start(f32[128]{0:T(128)} %param.16) | copy-start | bytes 1540
where the time goes:
time: 46 us; the launch traced here: 45.6 us
  Pallas kernels  35.6 us (77%)
  local copies, waits for them, and re-layouts  9.99 us (22%)
    pallas_call x1, Pallas kernels, local(): pl.pallas_call(functools.partial(kernel, gx, gy), out_shape=jax.ShapeDtyp...  35.6 us
    unnamed x21, local copies, waits for them, and re-layouts  9.99 us

commit v1 on v0

v1 whole, which is shorter than its diff:
```python
import functools

import jax
import jax.numpy as jnp
from jax import lax
from jax.experimental import pallas as pl
from jax.experimental.pallas import tpu as pltpu
from jax.sharding import PartitionSpec as P

MESH = pl.DeviceIdType.MESH
F32 = jnp.float32
BF16 = jnp.bfloat16

OFFSETS = [
    (ox, oy, oz)
    for ox in (-1, 0, 1)
    for oy in (-1, 0, 1)
    for oz in (-1, 0, 1)
    if (ox, oy, oz) != (0, 0, 0)
]
NUMBER = {offset: k for k, offset in enumerate(OFFSETS)}
SIDES = [(-1, 0), (1, 0), (0, -1), (0, 1)]
EDGES = [(-1, -1), (-1, 1), (1, -1), (1, 1)]
ALL = SIDES + EDGES


def edge_of(step, last):
    return last if step < 0 else 0


def kernel(
    gx,
    gy,
    cell_hbm,
    nbr_hbm,
    feat,
    w1,
    b1_hbm,
    w2,
    b2_hbm,
    wc,
    bc_hbm,
    wl,
    out,
    cell,
    nbr,
    b1,
    b2,
    bc,
    staged,
    field,
    hidden,
    coarse_field,
    side_src,
    edge_src,
    cside_src,
    cedge_src,
    zin,
    zhid,
    zx,
    zy,
    zc,
    w1p,
    w2p,
    wcv,
    wlv,
    total,
    send_side,
    send_edge,
    recv_side,
    recv_edge,
    csend_side,
    csend_edge,
    crecv_side,
    crecv_edge,
    local_sem,
    send_sem,
    recv_sem,
):
    mx = lax.axis_index("gx")
    my = lax.axis_index("gy")

    def device_at(ox, oy):
        return (lax.rem(mx + ox + gx, gx), lax.rem(my + oy + gy, gy))

    barrier = pltpu.get_barrier_semaphore()
    for ox, oy in ALL:
        pl.semaphore_signal(
            barrier, inc=1, device_id=device_at(ox, oy), device_id_type=MESH
        )

    pairs = [
        (feat, staged),
        (cell_hbm, cell),
        (nbr_hbm, nbr),
        (b1_hbm, b1),
        (w1, w1p.at[0:3, :, :, 0:128]),
        (w1, w1p.at[1:4, :, :, 128:256]),
        (w2, w2p.at[0:3, :, :, 0:128]),
        (w2, w2p.at[1:4, :, :, 128:256]),
        (b2_hbm, b2),
        (wc, wcv),
        (wl, wlv),
        (bc_hbm, bc),
    ]
    copies = [
        pltpu.make_async_copy(src, dst, local_sem.at[k])
        for k, (src, dst) in enumerate(pairs)
    ]
    for copy in copies:
        copy.start()

    for wp in (w1p, w2p):
        wp[3, :, :, 0:128] = jnp.zeros((3, 384, 128), BF16)
        wp[0, :, :, 128:256] = jnp.zeros((3, 384, 128), BF16)
    field[4] = jnp.zeros((4, 2, 8, 8, 128), F32)
    hidden[4] = jnp.zeros((4, 2, 8, 8, 128), F32)
    coarse_field[4] = jnp.zeros((4, 4, 8, 128), F32)
    for d in range(4):
        side_src[d, 8] = jnp.zeros((8, 8, 128), F32)
        cside_src[d, 8] = jnp.zeros((4, 8, 128), F32)
        edge_src[d, 16] = jnp.zeros((1, 8, 128), F32)
        cedge_src[d, 16] = jnp.zeros((1, 8, 128), F32)
    for z in (zin, zhid):
        z[:, :, 0] = jnp.zeros((2, 4, 32, 384), BF16)
        z[:, :, 9] = jnp.zeros((2, 4, 32, 384), BF16)
    zy[:, 0, 0] = jnp.zeros((2, 32, 384), BF16)
    zy[:, 1, 4] = jnp.zeros((2, 32, 384), BF16)

    copies[0].wait()
    for s in range(4):
        for x in range(8):
            field[s, x // 2, x % 2] = staged[s, x].astype(F32).reshape(8, 8, 128)

    def plane(source, s, x):
        if source is coarse_field:
            return source[s, x]
        return source[s, x // 2, x % 2]

    def across(source, s, y):
        if source is coarse_field:
            return source[s, :, y]
        return source[s, :, :, y].reshape(8, 8, 128)

    def column(source, s, x, y):
        if source is coarse_field:
            return source[s, x, y]
        return source[s, x // 2, x % 2, y]

    def exchange(number, source, last, sides, edges, rsides, redges):
        rows = 8 * (last + 1)
        for d, (ox, oy) in enumerate(SIDES):
            if number == 0 and oy == 0:
                continue
            for s in range(4):
                if oy == 0:
                    face = plane(source, s, edge_of(ox, last))
                else:
                    face = across(source, s, edge_of(oy, last))
                sides[d, s] = face.reshape(rows, 128).astype(BF16)
        for d, (ox, oy) in enumerate(EDGES):
            edges[d] = jnp.concatenate(
                [
                    column(source, s, edge_of(ox, last), edge_of(oy, last))
                    for s in range(4)
                ],
                axis=0,
            ).astype(BF16)
        described = []
        for k, (ox, oy) in enumerate(ALL):
            if k < 4:
                src, dst = sides.at[k], rsides.at[k]
                if number == 0 and oy == 0:
                    src = feat.at[:, edge_of(ox, last)]
            else:
                src, dst = edges.at[k - 4], redges.at[k - 4]
            described.append(
                pltpu.make_async_remote_copy(
                    src_ref=src,
                    dst_ref=dst,
                    send_sem=send_sem.at[number, k],
                    recv_sem=recv_sem.at[number, k],
                    device_id=device_at(-ox, -oy),
                    device_id_type=MESH,
                )
            )
        return described

    sent = exchange(
        0, field, 7, send_side.at[0], send_edge.at[0], recv_side.at[0], recv_edge.at[0]
    )
    pl.semaphore_wait(barrier, 8)
    for copy in sent:
        copy.start()

    for k in (1, 2, 3):
        copies[k].wait()
    live = [jnp.where(cell[s] >= 0, 1.0, 0.0).astype(F32) for s in range(4)]

    def index(s, ox, oy, oz):
        if (ox, oy, oz) == (0, 0, 0):
            return s
        entry = nbr[s, NUMBER[ox, oy, oz]]
        safe = jnp.maximum(entry, 0)
        block = lax.shift_right_logical(safe, 2)
        slot = lax.bitwise_and(safe, 3)
        if (ox, oy) == (0, 0):
            return jnp.where(entry < 0, 4, slot)
        if ox == 0 or oy == 0:
            place = slot + jnp.where(block == 4, 0, 4)
            return jnp.where(entry < 0, 8, place)
        beside_x = (ox + 1) * 3 + 1
        beside_y = 3 + (oy + 1)
        place = slot + jnp.where(
            block == 4,
            0,
            jnp.where(block == beside_x, 4, jnp.where(block == beside_y, 8, 12)),
        )
        return jnp.where(entry < 0, 16, place)

    where = {
        (s, ox, oy, oz): index(s, ox, oy, oz)
        for s in range(4)
        for ox in (-1, 0, 1)
        for oy in (-1, 0, 1)
        for oz in (-1, 0, 1)
    }

    def shifted(low, own, high, step):
        row = lax.broadcasted_iota(jnp.int32, own.shape, own.ndim - 2)
        axis = own.ndim - 2
        down = pltpu.roll(jnp.where(row >= 8 - step, low, own), step, axis)
        up = pltpu.roll(jnp.where(row < step, high, own), 8 - step, axis)
        return down, own, up

    def pair(fetch, ox, oy, step):
        for half in (0, 1):
            parts = [
                shifted(*[fetch(where[s, ox, oy, oz]) for oz in (-1, 0, 1)], step)
                for s in (2 * half, 2 * half + 1)
            ]
            for kz in range(3):
                both = jnp.concatenate([parts[0][kz], parts[1][kz]], axis=-2)
                yield slice(16 * half, 16 * half + 16), slice(
                    128 * kz, 128 * kz + 128
                ), both.astype(BF16)

    def fine_centre(source, z):
        def body(m, carry):
            for h in (0, 1):
                for rows, lanes, value in pair(lambda q: source[q, m, h], 0, 0, 1):
                    z[h, m, 1:9, rows, lanes] = value
            return carry

        lax.fori_loop(0, 4, body, 0)

    def fine_rim():
        for d, (ox, oy) in enumerate(SIDES):
            for rows, lanes, value in pair(lambda q: side_src[d, q], ox, oy, 1):
                if oy == 0:
                    zx[d, 1:9, rows, lanes] = value
                else:
                    split = value.reshape(4, 2, 16, 128)
                    zy[d - 2, 1, 0:4, rows, lanes] = split[:, 0]
                    zy[d - 2, 0, 1:5, rows, lanes] = split[:, 1]
        for d, (ox, oy) in enumerate(EDGES):
            for rows, lanes, value in pair(lambda q: edge_src[d, q], ox, oy, 1):
                zx[0 if ox < 0 else 1, 0 if oy < 0 else 9, rows, lanes] = value[0]

    def own_sources(source, last, sides, edges):
        for d, (ox, oy) in enumerate(SIDES):
            for s in range(4):
                if oy == 0:
                    sides[d, s] = plane(source, s, edge_of(ox, last))
                else:
                    sides[d, s] = across(source, s, edge_of(oy, last))
        for d, (ox, oy) in enumerate(EDGES):
            for s in range(4):
                edges[d, s, 0] = column(
                    source, s, edge_of(ox, last), edge_of(oy, last)
                )

    def received_sources(last, sides, edges, rsides, redges):
        for d in range(4):
            for s in range(4):
                sides[d, 4 + s] = rsides[d, s].astype(F32).reshape(last + 1, 8, 128)
        for d, (ox, oy) in enumerate(EDGES):
            dx = SIDES.index((ox, 0))
            dy = SIDES.index((0, oy))
            far = redges[d].astype(F32)
            for s in range(4):
                edges[d, 4 + s, 0] = sides[dx, 4 + s, edge_of(oy, last)]
                edges[d, 8 + s, 0] = sides[dy, 4 + s, edge_of(ox, last)]
                edges[d, 12 + s, 0] = far[8 * s : 8 * s + 8]

    def centre_conv(z, wp, i):
        planes = [(1, i - 1), (0, i), (1, i), (0, i + 1)]
        used = [p for p in range(4) if 0 <= planes[p][1] < 4]
        lhs = jnp.concatenate(
            [
                z[planes[p][0], planes[p][1], ky : ky + 8].reshape(256, 384)
                for ky in range(3)
                for p in used
            ],
            axis=1,
        )
        rhs = jnp.concatenate([wp[p, ky] for ky in range(3) for p in used], axis=0)
        return jnp.dot(lhs, rhs, preferred_element_type=F32)

    def convolve(z, wp, finish):
        for i in range(4):
            acc = centre_conv(z, wp, i)
            for h in (0, 1):
                part = acc[:, 128 * h : 128 * h + 128].reshape(8, 32, 128)
                total[i, h] = part
                if 0 < 2 * i + h < 7:
                    inner = part[1:7].reshape(6, 4, 8, 128)
                    for s in range(4):
                        finish(s, (i, h, slice(1, 7)), inner[:, s])

    def add_rim(wp, finish):
        for d in (0, 1):
            y, ky = (0, 0) if d == 0 else (7, 2)
            lhs = jnp.concatenate(
                [
                    zy[d, p % 2, p // 2 : p // 2 + 4].reshape(128, 384)
                    for p in range(4)
                ],
                axis=1,
            )
            rhs = jnp.concatenate([wp[p, ky] for p in range(4)], axis=0)
            add = jnp.dot(lhs, rhs, preferred_element_type=F32)
            for h in (0, 1):
                part = add[:, 128 * h : 128 * h + 128].reshape(4, 32, 128)
                part = total[:, h, y] + part
                if h == 0:
                    total[0, h, y] = part[0]
                else:
                    total[3, h, y] = part[3]
                inner = part.reshape(4, 4, 8, 128)
                for s in range(4):
                    finish(s, (slice(0, 4), h, y), inner[:, s])
        for d in (0, 1):
            i, h, p = (0, 0, 0) if d == 0 else (3, 1, 3)
            lhs = jnp.concatenate(
                [zx[d, ky : ky + 8].reshape(256, 384) for ky in range(3)], axis=1
            )
            rhs = jnp.concatenate(
                [wp[p, ky][:, 128 * h : 128 * h + 128] for ky in range(3)], axis=0
            )
            add = jnp.dot(lhs, rhs, preferred_element_type=F32).reshape(8, 32, 128)
            part = (total[i, h] + add).reshape(8, 4, 8, 128)
            for s in range(4):
                finish(s, (i, h, slice(0, 8)), part[:, s])

    own_sources(field, 7, side_src, edge_src)
    fine_centre(field, zin)

    copies[4].wait()
    copies[5].wait()

    def to_hidden(s, at, value):
        value = jnp.maximum(value + b1[...].reshape(1, 1, 128), 0.0) * live[s]
        hidden[(s,) + at] = value.astype(BF16).astype(F32)

    convolve(zin, w1p, to_hidden)
    for copy in sent:
        copy.wait_recv()
    received_sources(7, side_src, edge_src, recv_side.at[0], recv_edge.at[0])
    fine_rim()
    add_rim(w1p, to_hidden)
    sent_hidden = exchange(
        1, hidden, 7, send_side.at[1], send_edge.at[1], recv_side.at[1], recv_edge.at[1]
    )
    for copy in sent_hidden:
        copy.start()
    own_sources(hidden, 7, side_src, edge_src)
    fine_centre(hidden, zhid)

    for k in (6, 7, 8):
        copies[k].wait()

    def to_fine(s, at, value):
        value = value + b2[...].reshape(1, 1, 128) + field[(s,) + at]
        out[(s,) + at] = value * live[s]

    convolve(zhid, w2p, to_fine)
    for copy in sent_hidden:
        copy.wait_recv()
    received_sources(7, side_src, edge_src, recv_side.at[1], recv_edge.at[1])
    fine_rim()
    add_rim(w2p, to_fine)

    for s in range(4):
        for i in range(4):
            rows = (out[s, i, 0] + out[s, i, 1]).reshape(4, 2, 8, 128)
            rows = rows[:, 0] + rows[:, 1]
            even = lax.broadcasted_iota(jnp.int32, rows.shape, 1) % 2 == 0
            other = jnp.where(even, pltpu.roll(rows, 7, 1), pltpu.roll(rows, 1, 1))
            mean = (rows + other) * 0.125
            coarse_field[s, i] = mean.astype(BF16).astype(F32)
    sent_coarse = exchange(
        2, coarse_field, 3, csend_side, csend_edge, crecv_side, crecv_edge
    )
    for copy in sent_coarse:
        copy.start()
    own_sources(coarse_field, 3, cside_src, cedge_src)
    for x in range(4):
        for rows, lanes, value in pair(lambda q: coarse_field[q, x], 0, 0, 2):
            zc[x + 1, 1:5, rows, lanes] = value
    for k in (9, 10, 11):
        copies[k].wait()
    for copy in sent_coarse:
        copy.wait_recv()
    received_sources(3, cside_src, cedge_src, crecv_side, crecv_edge)
    for d, (ox, oy) in enumerate(SIDES):
        for rows, lanes, value in pair(lambda q: cside_src[d, q], ox, oy, 2):
            if oy == 0:
                zc[0 if ox < 0 else 5, 1:5, rows, lanes] = value
            else:
                zc[1:5, 0 if oy < 0 else 5, rows, lanes] = value
    for d, (ox, oy) in enumerate(EDGES):
        for rows, lanes, value in pair(lambda q: cedge_src[d, q], ox, oy, 2):
            zc[0 if ox < 0 else 5, 0 if oy < 0 else 5, rows, lanes] = value[0]

    lhs = jnp.concatenate(
        [
            zc[kx : kx + 4, ky : ky + 4].reshape(512, 384)
            for kx in range(3)
            for ky in range(3)
        ],
        axis=1,
    )
    acc = jnp.dot(lhs, wcv[...], preferred_element_type=F32)
    acc = jnp.maximum(acc + bc[...], 0.0).reshape(16, 4, 8, 256)
    acc = jnp.concatenate([(acc[:, s] * live[s])[:, None] for s in range(4)], axis=1)
    lifted = jnp.dot(
        acc.reshape(512, 256).astype(BF16), wlv[...], preferred_element_type=F32
    ).reshape(4, 4, 1, 4, 8, 128)
    for s in range(4):
        for x in range(4):
            raised = jnp.broadcast_to(lifted[x, :, :, s], (4, 2, 8, 128))
            raised = raised.reshape(8, 8, 128)
            for h in (0, 1):
                out[s, x, h] = (out[s, x, h] + raised) * live[s]
    for copy in sent + sent_hidden + sent_coarse:
        copy.wait_send()


def local(gx, gy, features, slot_cell, neighbours, w1, b1, w2, b2, wc, bc, wl):
    operands = [
        pltpu.with_memory_space_constraint(operand, pltpu.HBM)
        for operand in (
            slot_cell.reshape(4),
            neighbours.reshape(4, 26),
            features.reshape(4, 8, 64, 128),
            w1.reshape(3, 3, 384, 128),
            b1.reshape(1, 128),
            w2.reshape(3, 3, 384, 128),
            b2.reshape(1, 128),
            wc.reshape(3456, 256),
            bc.reshape(1, 256),
            wl,
        )
    ]
    result = pl.pallas_call(
        functools.partial(kernel, gx, gy),
        out_shape=jax.ShapeDtypeStruct((4, 4, 2, 8, 8, 128), F32),
        in_specs=[pl.BlockSpec(memory_space=pl.ANY)] * 10,
        out_specs=pl.BlockSpec(memory_space=pltpu.VMEM),
        scratch_shapes=[
            pltpu.SMEM((4,), jnp.int32),
            pltpu.SMEM((4, 26), jnp.int32),
            pltpu.VMEM((1, 128), F32),
            pltpu.VMEM((1, 128), F32),
            pltpu.VMEM((1, 256), F32),
            pltpu.VMEM((4, 8, 64, 128), BF16),
            pltpu.VMEM((5, 4, 2, 8, 8, 128), F32),
            pltpu.VMEM((5, 4, 2, 8, 8, 128), F32),
            pltpu.VMEM((5, 4, 4, 8, 128), F32),
            pltpu.VMEM((4, 9, 8, 8, 128), F32),
            pltpu.VMEM((4, 17, 1, 8, 128), F32),
            pltpu.VMEM((4, 9, 4, 8, 128), F32),
            pltpu.VMEM((4, 17, 1, 8, 128), F32),
            pltpu.VMEM((2, 4, 10, 32, 384), BF16),
            pltpu.VMEM((2, 4, 10, 32, 384), BF16),
            pltpu.VMEM((2, 10, 32, 384), BF16),
            pltpu.VMEM((2, 2, 5, 32, 384), BF16),
            pltpu.VMEM((6, 6, 32, 384), BF16),
            pltpu.VMEM((4, 3, 384, 256), BF16),
            pltpu.VMEM((4, 3, 384, 256), BF16),
            pltpu.VMEM((3456, 256), BF16),
            pltpu.VMEM((256, 128), BF16),
            pltpu.VMEM((4, 2, 8, 32, 128), F32),
            pltpu.VMEM((2, 4, 4, 64, 128), BF16),
            pltpu.VMEM((2, 4, 32, 128), BF16),
            pltpu.VMEM((2, 4, 4, 64, 128), BF16),
            pltpu.VMEM((2, 4, 32, 128), BF16),
            pltpu.VMEM((4, 4, 32, 128), BF16),
            pltpu.VMEM((4, 32, 128), BF16),
            pltpu.VMEM((4, 4, 32, 128), BF16),
            pltpu.VMEM((4, 32, 128), BF16),
            pltpu.SemaphoreType.DMA((12,)),
            pltpu.SemaphoreType.DMA((3, 8)),
            pltpu.SemaphoreType.DMA((3, 8)),
        ],
        compiler_params=pltpu.CompilerParams(
            collective_id=0, has_side_effects=True, vmem_limit_bytes=48 * 2**20
        ),
        cost_estimate=pl.CostEstimate(
            flops=8_000_000_000, bytes_accessed=8_000_000, transcendentals=0
        ),
        name="unet_window",
    )(*operands)
    return result.reshape(1, 1, 4, 512, 128)


def solution(mesh):
    placed = (
        P("gx", "gy", None, None, None),
        P("gx", "gy", None),
        P("gx", "gy", None, None),
    ) + (P(),) * 7
    return jax.shard_map(
        functools.partial(local, mesh.shape["gx"], mesh.shape["gy"]),
        mesh=mesh,
        in_specs=placed,
        out_specs=P("gx", "gy", None, None, None),
        check_vma=False,
    )
```

time: 46 us -> 28.6 us (0.62)
  local copies, waits for them, and re-layouts: 9.99 us -> 0.97 us
  Pallas kernels: 35.6 us -> 27.5 us
    unnamed x21 -> x1, local copies, waits for them, and re-layouts: 9.99 us -> 0.97 us
    pallas_call x1, Pallas kernels: 35.6 us -> 27.5 us  [local(): pl.pallas_call(functools.partial(kernel, gx, gy), out_shape=jax.ShapeDtyp...]
where the time goes in v1:
time: 28.6 us; the launch traced here: 28.5 us
  Pallas kernels  27.5 us (96%)
  local copies, waits for them, and re-layouts  0.97 us (3%)
    pallas_call x1, Pallas kernels, local(): pl.pallas_call(functools.partial(kernel, gx, gy), out_shape=jax.ShapeDtyp...  27.5 us
    unnamed x1, local copies, waits for them, and re-layouts  0.97 us

profile of v1, /device:TPU:1, one launch (start us, length us, event | category | flops | bytes accessed | tf_op | source)
XLA Modules:
  0.0 28.5 jit_solution(8772627421530366764)
XLA Ops:
  0.0 27.5 %unet_window.1 = f32[4,4,2,8,8,128]{5,4,3,2,1,0:T(8,128)S(1)} custom-call(s32[4]{0:T(128)} %bitcast.17, s32[4,26]{1,0:T(4,128)} %bitcast.15, bf16[4,8,64,128]{3,2,1,0:T(8,128)(2,1)} %bitcast.14, bf16[3,3,384,128]{3,2,1,0:T(8,128)(2,1)} %bitcast.12, f32[1,128]{1,0:T(1,128)} %bitcast.18, bf16[3,3,384,128]{3,2,1,0:T(8,128)(2,1)} %bitcast.13, ...), custom_call_target="tpu_custom_call" | custom-call | flops 8000000000 | bytes 8000000 | tf_op jit(solution)/shard_map/unet_window/pallas_call | solution.py:466
  27.5 1.0 %copy.12 = f32[1,1,4,512,128]{4,3,2,1,0:T(8,128)} copy(f32[1,1,4,512,128]{4,3,2,1,0:T(8,128)S(1)} %bitcast.10) | data formatting | bytes 2097152

commit v2 on v1

--- a/solution.py
+++ b/solution.py
@@ -107,7 +107,7 @@
         pltpu.make_async_copy(src, dst, local_sem.at[k])
         for k, (src, dst) in enumerate(pairs)
     ]
-    for copy in copies:
+    for copy in copies[:6]:
         copy.start()
 
     for wp in (w1p, w2p):
@@ -167,7 +167,8 @@
                 axis=0,
             ).astype(BF16)
         described = []
-        for k, (ox, oy) in enumerate(ALL):
+        for k in (4, 5, 6, 7, 2, 3, 0, 1):
+            ox, oy = ALL[k]
             if k < 4:
                 src, dst = sides.at[k], rsides.at[k]
                 if number == 0 and oy == 0:
@@ -358,6 +359,8 @@
 
     copies[4].wait()
     copies[5].wait()
+    for copy in copies[6:]:
+        copy.start()
 
     def to_hidden(s, at, value):
         value = jnp.maximum(value + b1[...].reshape(1, 1, 128), 0.0) * live[s]

time: 28.6 us -> 27 us (0.944)
  Pallas kernels: 27.5 us -> 25.9 us
    pallas_call x1, Pallas kernels: 27.5 us -> 25.9 us  [local(): pl.pallas_call(functools.partial(kernel, gx, gy), out_shape=jax.ShapeDtyp...]
where the time goes in v2:
time: 27 us; the launch traced here: 26.9 us
  Pallas kernels  25.9 us (96%)
  local copies, waits for them, and re-layouts  0.97 us (4%)
    pallas_call x1, Pallas kernels, local(): pl.pallas_call(functools.partial(kernel, gx, gy), out_shape=jax.ShapeDtyp...  25.9 us
    unnamed x1, local copies, waits for them, and re-layouts  0.97 us

profile of v2, /device:TPU:1, one launch (start us, length us, event | category | flops | bytes accessed | tf_op | source)
XLA Modules:
  0.0 26.9 jit_solution(11656486904289502120)
XLA Ops:
  0.0 25.9 %unet_window.1 = f32[4,4,2,8,8,128]{5,4,3,2,1,0:T(8,128)S(1)} custom-call(s32[4]{0:T(128)} %bitcast.17, s32[4,26]{1,0:T(4,128)} %bitcast.15, bf16[4,8,64,128]{3,2,1,0:T(8,128)(2,1)} %bitcast.14, bf16[3,3,384,128]{3,2,1,0:T(8,128)(2,1)} %bitcast.12, f32[1,128]{1,0:T(1,128)} %bitcast.18, bf16[3,3,384,128]{3,2,1,0:T(8,128)(2,1)} %bitcast.13, ...), custom_call_target="tpu_custom_call" | custom-call | flops 8000000000 | bytes 8000000 | tf_op jit(solution)/shard_map/unet_window/pallas_call | solution.py:469
  26.0 1.0 %copy.12 = f32[1,1,4,512,128]{4,3,2,1,0:T(8,128)} copy(f32[1,1,4,512,128]{4,3,2,1,0:T(8,128)S(1)} %bitcast.10) | data formatting | bytes 2097152

commit v3 on v2

--- a/solution.py
+++ b/solution.py
@@ -83,11 +83,30 @@
     def device_at(ox, oy):
         return (lax.rem(mx + ox + gx, gx), lax.rem(my + oy + gy, gy))
 
-    barrier = pltpu.get_barrier_semaphore()
-    for ox, oy in ALL:
+    def inside(ox, oy):
+        found = None
+        for at, step, size in ((mx, ox, gx), (my, oy, gy)):
+            if step != 0:
+                here = at > 0 if step < 0 else at < size - 1
+                found = here if found is None else jnp.logical_and(found, here)
+        return found
+
+    def when_inside(ox, oy, act):
+        @pl.when(inside(ox, oy))
+        def _():
+            act()
+
+    def signal_to(ox, oy):
         pl.semaphore_signal(
             barrier, inc=1, device_id=device_at(ox, oy), device_id_type=MESH
         )
+
+    barrier = pltpu.get_barrier_semaphore()
+    for ox, oy in ALL:
+        when_inside(ox, oy, functools.partial(signal_to, ox, oy))
+    beside_x = jnp.where(mx > 0, 1, 0) + jnp.where(mx < gx - 1, 1, 0)
+    beside_y = jnp.where(my > 0, 1, 0) + jnp.where(my < gy - 1, 1, 0)
+    partners = (1 + beside_x) * (1 + beside_y) - 1
 
     pairs = [
         (feat, staged),
@@ -166,7 +185,7 @@
                 ],
                 axis=0,
             ).astype(BF16)
-        described = []
+        described = {}
         for k in (4, 5, 6, 7, 2, 3, 0, 1):
             ox, oy = ALL[k]
             if k < 4:
@@ -175,7 +194,7 @@
                     src = feat.at[:, edge_of(ox, last)]
             else:
                 src, dst = edges.at[k - 4], redges.at[k - 4]
-            described.append(
+            described[ox, oy] = (
                 pltpu.make_async_remote_copy(
                     src_ref=src,
                     dst_ref=dst,
@@ -187,12 +206,19 @@
             )
         return described
 
+    def start(described):
+        for (ox, oy), copy in described.items():
+            when_inside(-ox, -oy, copy.start)
+
+    def arrive(described):
+        for (ox, oy), copy in described.items():
+            when_inside(ox, oy, copy.wait_recv)
+
     sent = exchange(
         0, field, 7, send_side.at[0], send_edge.at[0], recv_side.at[0], recv_edge.at[0]
     )
-    pl.semaphore_wait(barrier, 8)
-    for copy in sent:
-        copy.start()
+    pl.semaphore_wait(barrier, partners)
+    start(sent)
 
     for k in (1, 2, 3):
         copies[k].wait()
@@ -367,16 +393,14 @@
         hidden[(s,) + at] = value.astype(BF16).astype(F32)
 
     convolve(zin, w1p, to_hidden)
-    for copy in sent:
-        copy.wait_recv()
+    arrive(sent)
     received_sources(7, side_src, edge_src, recv_side.at[0], recv_edge.at[0])
     fine_rim()
     add_rim(w1p, to_hidden)
     sent_hidden = exchange(
         1, hidden, 7, send_side.at[1], send_edge.at[1], recv_side.at[1], recv_edge.at[1]
     )
-    for copy in sent_hidden:
-        copy.start()
+    start(sent_hidden)
     own_sources(hidden, 7, side_src, edge_src)
     fine_centre(hidden, zhid)
 
@@ -388,8 +412,7 @@
         out[(s,) + at] = value * live[s]
 
     convolve(zhid, w2p, to_fine)
-    for copy in sent_hidden:
-        copy.wait_recv()
+    arrive(sent_hidden)
     received_sources(7, side_src, edge_src, recv_side.at[1], recv_edge.at[1])
     fine_rim()
     add_rim(w2p, to_fine)
@@ -405,16 +428,14 @@
     sent_coarse = exchange(
         2, coarse_field, 3, csend_side, csend_edge, crecv_side, crecv_edge
     )
-    for copy in sent_coarse:
-        copy.start()
+    start(sent_coarse)
     own_sources(coarse_field, 3, cside_src, cedge_src)
     for x in range(4):
         for rows, lanes, value in pair(lambda q: coarse_field[q, x], 0, 0, 2):
             zc[x + 1, 1:5, rows, lanes] = value
     for k in (9, 10, 11):
         copies[k].wait()
-    for copy in sent_coarse:
-        copy.wait_recv()
+    arrive(sent_coarse)
     received_sources(3, cside_src, cedge_src, crecv_side, crecv_edge)
     for d, (ox, oy) in enumerate(SIDES):
         for rows, lanes, value in pair(lambda q: cside_src[d, q], ox, oy, 2):
@@ -446,8 +467,9 @@
             raised = raised.reshape(8, 8, 128)
             for h in (0, 1):
                 out[s, x, h] = (out[s, x, h] + raised) * live[s]
-    for copy in sent + sent_hidden + sent_coarse:
-        copy.wait_send()
+    for described in (sent, sent_hidden, sent_coarse):
+        for (ox, oy), copy in described.items():
+            when_inside(-ox, -oy, copy.wait_send)
 
 
 def local(gx, gy, features, slot_cell, neighbours, w1, b1, w2, b2, wc, bc, wl):

time: 27 us -> 21.8 us (0.81)
  the two profiles are of different devices: /device:TPU:1 before, /device:TPU:57 now
where the time goes in v3:
time: 21.8 us; the launch traced here: 21.7 us
  Pallas kernels  20.7 us (95%)
  local copies, waits for them, and re-layouts  0.97 us (4%)
    pallas_call x1, Pallas kernels, local(): pl.pallas_call(functools.partial(kernel, gx, gy), out_shape=jax.ShapeDtyp...  20.7 us
    unnamed x1, local copies, waits for them, and re-layouts  0.97 us

profile of v3, /device:TPU:57, one launch (start us, length us, event | category | flops | bytes accessed | tf_op | source)
XLA Modules:
  0.0 21.7 jit_solution(10379311739171811089)
XLA Ops:
  0.0 20.7 %unet_window.1 = f32[4,4,2,8,8,128]{5,4,3,2,1,0:T(8,128)S(1)} custom-call(s32[4]{0:T(128)} %bitcast.17, s32[4,26]{1,0:T(4,128)} %bitcast.15, bf16[4,8,64,128]{3,2,1,0:T(8,128)(2,1)} %bitcast.14, bf16[3,3,384,128]{3,2,1,0:T(8,128)(2,1)} %bitcast.12, f32[1,128]{1,0:T(1,128)} %bitcast.18, bf16[3,3,384,128]{3,2,1,0:T(8,128)(2,1)} %bitcast.13, ...), custom_call_target="tpu_custom_call" | custom-call | flops 8000000000 | bytes 8000000 | tf_op jit(solution)/shard_map/unet_window/pallas_call | solution.py:491
  20.7 1.0 %copy.12 = f32[1,1,4,512,128]{4,3,2,1,0:T(8,128)} copy(f32[1,1,4,512,128]{4,3,2,1,0:T(8,128)S(1)} %bitcast.10) | data formatting | bytes 2097152

commit v4 on v3

--- a/solution.py
+++ b/solution.py
@@ -22,6 +22,7 @@
 SIDES = [(-1, 0), (1, 0), (0, -1), (0, 1)]
 EDGES = [(-1, -1), (-1, 1), (1, -1), (1, 1)]
 ALL = SIDES + EDGES
+FARTHEST = (4, 5, 6, 7, 2, 3, 0, 1)
 
 
 def edge_of(step, last):
@@ -48,6 +49,7 @@
     b2,
     bc,
     staged,
+    staged_rim,
     field,
     hidden,
     coarse_field,
@@ -60,11 +62,14 @@
     zx,
     zy,
     zc,
+    zcx,
+    zcy,
     w1p,
     w2p,
     wcv,
     wlv,
     total,
+    ctotal,
     send_side,
     send_edge,
     recv_side,
@@ -74,6 +79,7 @@
     crecv_side,
     crecv_edge,
     local_sem,
+    rim_sem,
     send_sem,
     recv_sem,
 ):
@@ -102,8 +108,8 @@
         )
 
     barrier = pltpu.get_barrier_semaphore()
-    for ox, oy in ALL:
-        when_inside(ox, oy, functools.partial(signal_to, ox, oy))
+    for k in FARTHEST:
+        when_inside(*ALL[k], functools.partial(signal_to, *ALL[k]))
     beside_x = jnp.where(mx > 0, 1, 0) + jnp.where(mx < gx - 1, 1, 0)
     beside_y = jnp.where(my > 0, 1, 0) + jnp.where(my < gy - 1, 1, 0)
     partners = (1 + beside_x) * (1 + beside_y) - 1
@@ -126,7 +132,13 @@
         pltpu.make_async_copy(src, dst, local_sem.at[k])
         for k, (src, dst) in enumerate(pairs)
     ]
-    for copy in copies[:6]:
+    rims = [
+        pltpu.make_async_copy(
+            feat.at[:, :, 48 * d : 48 * d + 16], staged_rim.at[d], rim_sem.at[d]
+        )
+        for d in (0, 1)
+    ]
+    for copy in rims + copies[:6]:
         copy.start()
 
     for wp in (w1p, w2p):
@@ -143,13 +155,17 @@
     for z in (zin, zhid):
         z[:, :, 0] = jnp.zeros((2, 4, 32, 384), BF16)
         z[:, :, 9] = jnp.zeros((2, 4, 32, 384), BF16)
-    zy[:, 0, 0] = jnp.zeros((2, 32, 384), BF16)
-    zy[:, 1, 4] = jnp.zeros((2, 32, 384), BF16)
-
-    copies[0].wait()
-    for s in range(4):
-        for x in range(8):
-            field[s, x // 2, x % 2] = staged[s, x].astype(F32).reshape(8, 8, 128)
+    for side in range(2):
+        for end in (0, 9):
+            zx[side, end] = jnp.zeros((32, 384), BF16)
+        for end in (0, 5):
+            zcx[side, end] = jnp.zeros((32, 384), BF16)
+    for end in (0, 5):
+        zc[end] = jnp.zeros((6, 32, 384), BF16)
+        zc[:, end] = jnp.zeros((6, 32, 384), BF16)
+
+    for copy in rims:
+        copy.wait()
 
     def plane(source, s, x):
         if source is coarse_field:
@@ -159,11 +175,17 @@
     def across(source, s, y):
         if source is coarse_field:
             return source[s, :, y]
+        if source is field:
+            d = y // 7
+            return staged_rim[d, s].astype(F32)[:, 8 * d : 8 * d + 8]
         return source[s, :, :, y].reshape(8, 8, 128)
 
     def column(source, s, x, y):
         if source is coarse_field:
             return source[s, x, y]
+        if source is field:
+            d = y // 7
+            return staged_rim[d, s, x].astype(F32)[8 * d : 8 * d + 8]
         return source[s, x // 2, x % 2, y]
 
     def exchange(number, source, last, sides, edges, rsides, redges):
@@ -186,7 +208,7 @@
                 axis=0,
             ).astype(BF16)
         described = {}
-        for k in (4, 5, 6, 7, 2, 3, 0, 1):
+        for k in FARTHEST:
             ox, oy = ALL[k]
             if k < 4:
                 src, dst = sides.at[k], rsides.at[k]
@@ -210,15 +232,20 @@
         for (ox, oy), copy in described.items():
             when_inside(-ox, -oy, copy.start)
 
-    def arrive(described):
-        for (ox, oy), copy in described.items():
-            when_inside(ox, oy, copy.wait_recv)
+    def arrive(described, directions):
+        for ox, oy in directions:
+            when_inside(ox, oy, described[ox, oy].wait_recv)
 
     sent = exchange(
         0, field, 7, send_side.at[0], send_edge.at[0], recv_side.at[0], recv_edge.at[0]
     )
     pl.semaphore_wait(barrier, partners)
     start(sent)
+
+    copies[0].wait()
+    for s in range(4):
+        for x in range(8):
+            field[s, x // 2, x % 2] = staged[s, x].astype(F32).reshape(8, 8, 128)
 
     for k in (1, 2, 3):
         copies[k].wait()
@@ -281,18 +308,23 @@
 
         lax.fori_loop(0, 4, body, 0)
 
-    def fine_rim():
-        for d, (ox, oy) in enumerate(SIDES):
-            for rows, lanes, value in pair(lambda q: side_src[d, q], ox, oy, 1):
-                if oy == 0:
-                    zx[d, 1:9, rows, lanes] = value
-                else:
-                    split = value.reshape(4, 2, 16, 128)
-                    zy[d - 2, 1, 0:4, rows, lanes] = split[:, 0]
-                    zy[d - 2, 0, 1:5, rows, lanes] = split[:, 1]
-        for d, (ox, oy) in enumerate(EDGES):
-            for rows, lanes, value in pair(lambda q: edge_src[d, q], ox, oy, 1):
-                zx[0 if ox < 0 else 1, 0 if oy < 0 else 9, rows, lanes] = value[0]
+    def x_rim(number, sides, low, high):
+        for d in (0, 1):
+            for rows, lanes, value in pair(lambda q: sides[d, q], *SIDES[d], number):
+                low[d, 1 : high + 1, rows, lanes] = value
+
+    def fine_y_rim():
+        for d in (0, 1):
+            for rows, lanes, value in pair(
+                lambda q: side_src[d + 2, q], *SIDES[d + 2], 1
+            ):
+                split = value.reshape(4, 2, 16, 128)
+                zy[d, 1, 0:4, rows, lanes] = split[:, 0]
+                zy[d, 0, 1:5, rows, lanes] = split[:, 1]
+        for k, (ox, oy) in enumerate(EDGES):
+            at = (0, 0) if ox < 0 else (1, 4)
+            for rows, lanes, value in pair(lambda q: edge_src[k, q], ox, oy, 1):
+                zy[(0 if oy < 0 else 1,) + at + (rows, lanes)] = value[0]
 
     def own_sources(source, last, sides, edges):
         for d, (ox, oy) in enumerate(SIDES):
@@ -307,10 +339,12 @@
                     source, s, edge_of(ox, last), edge_of(oy, last)
                 )
 
-    def received_sources(last, sides, edges, rsides, redges):
-        for d in range(4):
+    def received_sides(which, last, sides, rsides):
+        for d in which:
             for s in range(4):
                 sides[d, 4 + s] = rsides[d, s].astype(F32).reshape(last + 1, 8, 128)
+
+    def received_edges(last, sides, edges, redges):
         for d, (ox, oy) in enumerate(EDGES):
             dx = SIDES.index((ox, 0))
             dy = SIDES.index((0, oy))
@@ -345,7 +379,31 @@
                     for s in range(4):
                         finish(s, (i, h, slice(1, 7)), inner[:, s])
 
-    def add_rim(wp, finish):
+    def add_x(number, described, wp, finish):
+        arrive(described, SIDES[:2])
+        received_sides((0, 1), 7, side_src, recv_side.at[number])
+        x_rim(1, side_src, zx, 8)
+        for d in (0, 1):
+            i, h, p = (0, 0, 0) if d == 0 else (3, 1, 3)
+            lhs = jnp.concatenate(
+                [zx[d, ky : ky + 8].reshape(256, 384) for ky in range(3)], axis=1
+            )
+            rhs = jnp.concatenate(
+                [wp[p, ky][:, 128 * h : 128 * h + 128] for ky in range(3)], axis=0
+            )
+            add = jnp.dot(lhs, rhs, preferred_element_type=F32).reshape(8, 32, 128)
+            part = total[i, h] + add
+            for y in (0, 7):
+                total[i, h, y] = part[y]
+            inner = part[1:7].reshape(6, 4, 8, 128)
+            for s in range(4):
+                finish(s, (i, h, slice(1, 7)), inner[:, s])
+
+    def add_y(number, described, wp, finish):
+        arrive(described, EDGES + SIDES[2:])
+        received_sides((2, 3), 7, side_src, recv_side.at[number])
+        received_edges(7, side_src, edge_src, recv_edge.at[number])
+        fine_y_rim()
         for d in (0, 1):
             y, ky = (0, 0) if d == 0 else (7, 2)
             lhs = jnp.concatenate(
@@ -359,26 +417,9 @@
             add = jnp.dot(lhs, rhs, preferred_element_type=F32)
             for h in (0, 1):
                 part = add[:, 128 * h : 128 * h + 128].reshape(4, 32, 128)
-                part = total[:, h, y] + part
-                if h == 0:
-                    total[0, h, y] = part[0]
-                else:
-                    total[3, h, y] = part[3]
-                inner = part.reshape(4, 4, 8, 128)
+                part = (total[:, h, y] + part).reshape(4, 4, 8, 128)
                 for s in range(4):
-                    finish(s, (slice(0, 4), h, y), inner[:, s])
-        for d in (0, 1):
-            i, h, p = (0, 0, 0) if d == 0 else (3, 1, 3)
-            lhs = jnp.concatenate(
-                [zx[d, ky : ky + 8].reshape(256, 384) for ky in range(3)], axis=1
-            )
-            rhs = jnp.concatenate(
-                [wp[p, ky][:, 128 * h : 128 * h + 128] for ky in range(3)], axis=0
-            )
-            add = jnp.dot(lhs, rhs, preferred_element_type=F32).reshape(8, 32, 128)
-            part = (total[i, h] + add).reshape(8, 4, 8, 128)
-            for s in range(4):
-                finish(s, (i, h, slice(0, 8)), part[:, s])
+                    finish(s, (slice(0, 4), h, y), part[:, s])
 
     own_sources(field, 7, side_src, edge_src)
     fine_centre(field, zin)
@@ -393,10 +434,8 @@
         hidden[(s,) + at] = value.astype(BF16).astype(F32)
 
     convolve(zin, w1p, to_hidden)
-    arrive(sent)
-    received_sources(7, side_src, edge_src, recv_side.at[0], recv_edge.at[0])
-    fine_rim()
-    add_rim(w1p, to_hidden)
+    add_x(0, sent, w1p, to_hidden)
+    add_y(0, sent, w1p, to_hidden)
     sent_hidden = exchange(
         1, hidden, 7, send_side.at[1], send_edge.at[1], recv_side.at[1], recv_edge.at[1]
     )
@@ -411,42 +450,34 @@
         value = value + b2[...].reshape(1, 1, 128) + field[(s,) + at]
         out[(s,) + at] = value * live[s]
 
+    def pooled(value):
+        even = lax.broadcasted_iota(jnp.int32, value.shape, 1) % 2 == 0
+        other = jnp.where(even, pltpu.roll(value, 7, 1), pltpu.roll(value, 1, 1))
+        return ((value + other) * 0.125).astype(BF16).astype(F32)
+
+    def pool(ys):
+        for s in range(4):
+            for y in ys:
+                value = out[s, :, 0, 2 * y] + out[s, :, 1, 2 * y]
+                value = value + out[s, :, 0, 2 * y + 1] + out[s, :, 1, 2 * y + 1]
+                coarse_field[s, :, y] = pooled(value)
+
     convolve(zhid, w2p, to_fine)
-    arrive(sent_hidden)
-    received_sources(7, side_src, edge_src, recv_side.at[1], recv_edge.at[1])
-    fine_rim()
-    add_rim(w2p, to_fine)
-
-    for s in range(4):
-        for i in range(4):
-            rows = (out[s, i, 0] + out[s, i, 1]).reshape(4, 2, 8, 128)
-            rows = rows[:, 0] + rows[:, 1]
-            even = lax.broadcasted_iota(jnp.int32, rows.shape, 1) % 2 == 0
-            other = jnp.where(even, pltpu.roll(rows, 7, 1), pltpu.roll(rows, 1, 1))
-            mean = (rows + other) * 0.125
-            coarse_field[s, i] = mean.astype(BF16).astype(F32)
+    add_x(1, sent_hidden, w2p, to_fine)
+    pool((1, 2))
+    add_y(1, sent_hidden, w2p, to_fine)
+    pool((0, 3))
     sent_coarse = exchange(
         2, coarse_field, 3, csend_side, csend_edge, crecv_side, crecv_edge
     )
     start(sent_coarse)
+
     own_sources(coarse_field, 3, cside_src, cedge_src)
     for x in range(4):
         for rows, lanes, value in pair(lambda q: coarse_field[q, x], 0, 0, 2):
             zc[x + 1, 1:5, rows, lanes] = value
     for k in (9, 10, 11):
         copies[k].wait()
-    arrive(sent_coarse)
-    received_sources(3, cside_src, cedge_src, crecv_side, crecv_edge)
-    for d, (ox, oy) in enumerate(SIDES):
-        for rows, lanes, value in pair(lambda q: cside_src[d, q], ox, oy, 2):
-            if oy == 0:
-                zc[0 if ox < 0 else 5, 1:5, rows, lanes] = value
-            else:
-                zc[1:5, 0 if oy < 0 else 5, rows, lanes] = value
-    for d, (ox, oy) in enumerate(EDGES):
-        for rows, lanes, value in pair(lambda q: cedge_src[d, q], ox, oy, 2):
-            zc[0 if ox < 0 else 5, 0 if oy < 0 else 5, rows, lanes] = value[0]
-
     lhs = jnp.concatenate(
         [
             zc[kx : kx + 4, ky : ky + 4].reshape(512, 384)
@@ -456,17 +487,62 @@
         axis=1,
     )
     acc = jnp.dot(lhs, wcv[...], preferred_element_type=F32)
-    acc = jnp.maximum(acc + bc[...], 0.0).reshape(16, 4, 8, 256)
-    acc = jnp.concatenate([(acc[:, s] * live[s])[:, None] for s in range(4)], axis=1)
-    lifted = jnp.dot(
-        acc.reshape(512, 256).astype(BF16), wlv[...], preferred_element_type=F32
-    ).reshape(4, 4, 1, 4, 8, 128)
-    for s in range(4):
-        for x in range(4):
-            raised = jnp.broadcast_to(lifted[x, :, :, s], (4, 2, 8, 128))
-            raised = raised.reshape(8, 8, 128)
-            for h in (0, 1):
-                out[s, x, h] = (out[s, x, h] + raised) * live[s]
+    ctotal[...] = acc.reshape(4, 4, 32, 256)
+
+    def join(ys):
+        acc = jnp.concatenate([ctotal[:, y] for y in ys], axis=0)
+        acc = jnp.maximum(acc.reshape(-1, 256) + bc[...], 0.0)
+        acc = acc.reshape(4 * len(ys), 4, 8, 256)
+        acc = jnp.concatenate(
+            [(acc[:, s] * live[s])[:, None] for s in range(4)], axis=1
+        )
+        lifted = jnp.dot(
+            acc.reshape(-1, 256).astype(BF16), wlv[...], preferred_element_type=F32
+        ).reshape(len(ys), 4, 4, 8, 128)
+        for k, y in enumerate(ys):
+            for s in range(4):
+                raised = lifted[k, :, s]
+                for h in (0, 1):
+                    for f in (0, 1):
+                        at = (s, slice(0, 4), h, 2 * y + f)
+                        out[at] = (out[at] + raised) * live[s]
+
+    arrive(sent_coarse, SIDES[:2])
+    received_sides((0, 1), 3, cside_src, crecv_side)
+    x_rim(2, cside_src, zcx, 4)
+    for d in (0, 1):
+        lhs = jnp.concatenate(
+            [zcx[d, ky : ky + 4].reshape(128, 384) for ky in range(3)], axis=1
+        )
+        rhs = wcv[2304 * d : 2304 * d + 1152]
+        add = jnp.dot(lhs, rhs, preferred_element_type=F32)
+        ctotal[3 * d] = ctotal[3 * d] + add.reshape(4, 32, 256)
+    join((1, 2))
+    arrive(sent_coarse, EDGES + SIDES[2:])
+    received_sides((2, 3), 3, cside_src, crecv_side)
+    received_edges(3, cside_src, cedge_src, crecv_edge)
+    for d in (0, 1):
+        for rows, lanes, value in pair(
+            lambda q: cside_src[d + 2, q], *SIDES[d + 2], 2
+        ):
+            zcy[d, 1:5, rows, lanes] = value
+    for k, (ox, oy) in enumerate(EDGES):
+        for rows, lanes, value in pair(lambda q: cedge_src[k, q], ox, oy, 2):
+            zcy[0 if oy < 0 else 1, 0 if ox < 0 else 5, rows, lanes] = value[0]
+    for d in (0, 1):
+        lhs = jnp.concatenate(
+            [zcy[d, kx : kx + 4].reshape(128, 384) for kx in range(3)], axis=1
+        )
+        rhs = jnp.concatenate(
+            [
+                wcv[1152 * kx + 768 * d : 1152 * kx + 768 * d + 384]
+                for kx in range(3)
+            ],
+            axis=0,
+        )
+        add = jnp.dot(lhs, rhs, preferred_element_type=F32)
+        ctotal[:, 3 * d] = ctotal[:, 3 * d] + add.reshape(4, 32, 256)
+    join((0, 3))
     for described in (sent, sent_hidden, sent_coarse):
         for (ox, oy), copy in described.items():
             when_inside(-ox, -oy, copy.wait_send)
@@ -500,6 +576,7 @@
             pltpu.VMEM((1, 128), F32),
             pltpu.VMEM((1, 256), F32),
             pltpu.VMEM((4, 8, 64, 128), BF16),
+            pltpu.VMEM((2, 4, 8, 16, 128), BF16),
             pltpu.VMEM((5, 4, 2, 8, 8, 128), F32),
             pltpu.VMEM((5, 4, 2, 8, 8, 128), F32),
             pltpu.VMEM((5, 4, 4, 8, 128), F32),
@@ -512,11 +589,14 @@
             pltpu.VMEM((2, 10, 32, 384), BF16),
             pltpu.VMEM((2, 2, 5, 32, 384), BF16),
             pltpu.VMEM((6, 6, 32, 384), BF16),
+            pltpu.VMEM((2, 6, 32, 384), BF16),
+            pltpu.VMEM((2, 6, 32, 384), BF16),
             pltpu.VMEM((4, 3, 384, 256), BF16),
             pltpu.VMEM((4, 3, 384, 256), BF16),
             pltpu.VMEM((3456, 256), BF16),
             pltpu.VMEM((256, 128), BF16),
             pltpu.VMEM((4, 2, 8, 32, 128), F32),
+            pltpu.VMEM((4, 4, 32, 256), F32),
             pltpu.VMEM((2, 4, 4, 64, 128), BF16),
             pltpu.VMEM((2, 4, 32, 128), BF16),
             pltpu.VMEM((2, 4, 4, 64, 128), BF16),
@@ -526,6 +606,7 @@
             pltpu.VMEM((4, 4, 32, 128), BF16),
             pltpu.VMEM((4, 32, 128), BF16),
             pltpu.SemaphoreType.DMA((12,)),
+            pltpu.SemaphoreType.DMA((2,)),
             pltpu.SemaphoreType.DMA((3, 8)),
             pltpu.SemaphoreType.DMA((3, 8)),
         ],

time: 21.8 us -> 21.5 us (0.986)
  Pallas kernels: 20.7 us -> 20.2 us
    pallas_call x1, Pallas kernels: 20.7 us -> 20.2 us  [local(): pl.pallas_call(functools.partial(kernel, gx, gy), out_shape=jax.ShapeDtyp...]
where the time goes in v4:
time: 21.5 us; the launch traced here: 21.2 us
  Pallas kernels  20.2 us (94%)
  local copies, waits for them, and re-layouts  0.97 us (5%)
    pallas_call x1, Pallas kernels, local(): pl.pallas_call(functools.partial(kernel, gx, gy), out_shape=jax.ShapeDtyp...  20.2 us
    unnamed x1, local copies, waits for them, and re-layouts  0.97 us

profile of v4, /device:TPU:57, one launch (start us, length us, event | category | flops | bytes accessed | tf_op | source)
XLA Modules:
  0.0 21.2 jit_solution(5001000086539353137)
XLA Ops:
  0.0 20.2 %unet_window.1 = f32[4,4,2,8,8,128]{5,4,3,2,1,0:T(8,128)S(1)} custom-call(s32[4]{0:T(128)} %bitcast.17, s32[4,26]{1,0:T(4,128)} %bitcast.15, bf16[4,8,64,128]{3,2,1,0:T(8,128)(2,1)} %bitcast.14, bf16[3,3,384,128]{3,2,1,0:T(8,128)(2,1)} %bitcast.12, f32[1,128]{1,0:T(1,128)} %bitcast.18, bf16[3,3,384,128]{3,2,1,0:T(8,128)(2,1)} %bitcast.13, ...), custom_call_target="tpu_custom_call" | custom-call | flops 8000000000 | bytes 8000000 | tf_op jit(solution)/shard_map/unet_window/pallas_call | solution.py:567
  20.2 1.0 %copy.12 = f32[1,1,4,512,128]{4,3,2,1,0:T(8,128)} copy(f32[1,1,4,512,128]{4,3,2,1,0:T(8,128)S(1)} %bitcast.10) | data formatting | bytes 2097152

commit v5 on v4

--- a/solution.py
+++ b/solution.py
@@ -53,9 +53,7 @@
     field,
     hidden,
     coarse_field,
-    side_src,
     edge_src,
-    cside_src,
     cedge_src,
     zin,
     zhid,
@@ -70,19 +68,17 @@
     wlv,
     total,
     ctotal,
-    send_side,
     send_edge,
-    recv_side,
     recv_edge,
-    csend_side,
     csend_edge,
-    crecv_side,
     crecv_edge,
     local_sem,
     rim_sem,
     send_sem,
     recv_sem,
+    *side_refs,
 ):
+    sides = [side_refs[4 * number : 4 * number + 4] for number in range(3)]
     mx = lax.axis_index("gx")
     my = lax.axis_index("gy")
 
@@ -148,8 +144,8 @@
     hidden[4] = jnp.zeros((4, 2, 8, 8, 128), F32)
     coarse_field[4] = jnp.zeros((4, 4, 8, 128), F32)
     for d in range(4):
-        side_src[d, 8] = jnp.zeros((8, 8, 128), F32)
-        cside_src[d, 8] = jnp.zeros((4, 8, 128), F32)
+        for number, rows in ((0, 64), (1, 64), (2, 32)):
+            sides[number][d][8] = jnp.zeros((rows, 128), BF16)
         edge_src[d, 16] = jnp.zeros((1, 8, 128), F32)
         cedge_src[d, 16] = jnp.zeros((1, 8, 128), F32)
     for z in (zin, zhid):
@@ -188,17 +184,16 @@
             return staged_rim[d, s, x].astype(F32)[8 * d : 8 * d + 8]
         return source[s, x // 2, x % 2, y]
 
-    def exchange(number, source, last, sides, edges, rsides, redges):
-        rows = 8 * (last + 1)
-        for d, (ox, oy) in enumerate(SIDES):
-            if number == 0 and oy == 0:
-                continue
-            for s in range(4):
-                if oy == 0:
-                    face = plane(source, s, edge_of(ox, last))
-                else:
-                    face = across(source, s, edge_of(oy, last))
-                sides[d, s] = face.reshape(rows, 128).astype(BF16)
+    def pack_side(number, source, last, d):
+        ox, oy = SIDES[d]
+        for s in range(4):
+            if oy == 0:
+                face = plane(source, s, edge_of(ox, last))
+            else:
+                face = across(source, s, edge_of(oy, last))
+            sides[number][d][s] = face.reshape(8 * (last + 1), 128).astype(BF16)
+
+    def pack_edges(source, last, edges):
         for d, (ox, oy) in enumerate(EDGES):
             edges[d] = jnp.concatenate(
                 [
@@ -207,45 +202,59 @@
                 ],
                 axis=0,
             ).astype(BF16)
+
+    def describe(number, edges, redges):
         described = {}
         for k in FARTHEST:
             ox, oy = ALL[k]
             if k < 4:
-                src, dst = sides.at[k], rsides.at[k]
+                src = sides[number][k].at[0:4]
+                dst = sides[number][k].at[4:8]
                 if number == 0 and oy == 0:
-                    src = feat.at[:, edge_of(ox, last)]
+                    src = feat.at[:, edge_of(ox, 7)]
             else:
                 src, dst = edges.at[k - 4], redges.at[k - 4]
-            described[ox, oy] = (
-                pltpu.make_async_remote_copy(
-                    src_ref=src,
-                    dst_ref=dst,
-                    send_sem=send_sem.at[number, k],
-                    recv_sem=recv_sem.at[number, k],
-                    device_id=device_at(-ox, -oy),
-                    device_id_type=MESH,
-                )
+            described[ox, oy] = pltpu.make_async_remote_copy(
+                src_ref=src,
+                dst_ref=dst,
+                send_sem=send_sem.at[number, k],
+                recv_sem=recv_sem.at[number, k],
+                device_id=device_at(-ox, -oy),
+                device_id_type=MESH,
             )
         return described
 
-    def start(described):
-        for (ox, oy), copy in described.items():
-            when_inside(-ox, -oy, copy.start)
+    def start(described, directions):
+        for ox, oy in directions:
+            when_inside(-ox, -oy, described[ox, oy].start)
+
+    def exchange(number, source, last, edges, redges):
+        described = describe(number, edges, redges)
+        pack_edges(source, last, edges)
+        for d in (2, 3):
+            pack_side(number, source, last, d)
+        start(described, EDGES + SIDES[2:])
+        for d in (0, 1):
+            pack_side(number, source, last, d)
+        start(described, SIDES[:2])
+        return described
 
     def arrive(described, directions):
         for ox, oy in directions:
             when_inside(ox, oy, described[ox, oy].wait_recv)
 
-    sent = exchange(
-        0, field, 7, send_side.at[0], send_edge.at[0], recv_side.at[0], recv_edge.at[0]
-    )
+    sent = describe(0, send_edge.at[0], recv_edge.at[0])
+    pack_edges(field, 7, send_edge.at[0])
+    for d in (2, 3):
+        pack_side(0, field, 7, d)
     pl.semaphore_wait(barrier, partners)
-    start(sent)
-
+    start(sent, EDGES + SIDES[2:] + SIDES[:2])
     copies[0].wait()
     for s in range(4):
         for x in range(8):
             field[s, x // 2, x % 2] = staged[s, x].astype(F32).reshape(8, 8, 128)
+        for d in (0, 1):
+            sides[0][d][s] = staged[s, edge_of(SIDES[d][0], 7)]
 
     for k in (1, 2, 3):
         copies[k].wait()
@@ -308,51 +317,54 @@
 
         lax.fori_loop(0, 4, body, 0)
 
-    def x_rim(number, sides, low, high):
-        for d in (0, 1):
-            for rows, lanes, value in pair(lambda q: sides[d, q], *SIDES[d], number):
-                low[d, 1 : high + 1, rows, lanes] = value
-
-    def fine_y_rim():
-        for d in (0, 1):
-            for rows, lanes, value in pair(
-                lambda q: side_src[d + 2, q], *SIDES[d + 2], 1
-            ):
-                split = value.reshape(4, 2, 16, 128)
-                zy[d, 1, 0:4, rows, lanes] = split[:, 0]
-                zy[d, 0, 1:5, rows, lanes] = split[:, 1]
-        for k, (ox, oy) in enumerate(EDGES):
-            at = (0, 0) if ox < 0 else (1, 4)
-            for rows, lanes, value in pair(lambda q: edge_src[k, q], ox, oy, 1):
-                zy[(0 if oy < 0 else 1,) + at + (rows, lanes)] = value[0]
-
-    def own_sources(source, last, sides, edges):
-        for d, (ox, oy) in enumerate(SIDES):
-            for s in range(4):
-                if oy == 0:
-                    sides[d, s] = plane(source, s, edge_of(ox, last))
-                else:
-                    sides[d, s] = across(source, s, edge_of(oy, last))
+    def face(number, d):
+        def fetch(q):
+            value = sides[number][d][q].astype(F32)
+            return value.reshape(value.shape[0] // 8, 8, 128)
+
+        return fetch
+
+    def own_edges(source, last, edges):
         for d, (ox, oy) in enumerate(EDGES):
             for s in range(4):
                 edges[d, s, 0] = column(
                     source, s, edge_of(ox, last), edge_of(oy, last)
                 )
 
-    def received_sides(which, last, sides, rsides):
-        for d in which:
+    def end_of(number, d, s, step):
+        ref = sides[number][d]
+        if step < 0:
+            rows = ref.shape[1]
+            return ref[4 + s, rows - 16 : rows].astype(F32)[8:16]
+        return ref[4 + s, 0:16].astype(F32)[0:8]
+
+    def edges_beside_x(number, edges):
+        for k, (ox, oy) in enumerate(EDGES):
             for s in range(4):
-                sides[d, 4 + s] = rsides[d, s].astype(F32).reshape(last + 1, 8, 128)
-
-    def received_edges(last, sides, edges, redges):
-        for d, (ox, oy) in enumerate(EDGES):
-            dx = SIDES.index((ox, 0))
-            dy = SIDES.index((0, oy))
-            far = redges[d].astype(F32)
+                edges[k, 4 + s, 0] = end_of(number, SIDES.index((ox, 0)), s, oy)
+
+    def edges_beside_y(number, edges, redges):
+        for k, (ox, oy) in enumerate(EDGES):
+            far = redges[k].astype(F32)
             for s in range(4):
-                edges[d, 4 + s, 0] = sides[dx, 4 + s, edge_of(oy, last)]
-                edges[d, 8 + s, 0] = sides[dy, 4 + s, edge_of(ox, last)]
-                edges[d, 12 + s, 0] = far[8 * s : 8 * s + 8]
+                edges[k, 8 + s, 0] = end_of(number, SIDES.index((0, oy)), s, ox)
+                edges[k, 12 + s, 0] = far[8 * s : 8 * s + 8]
+
+    def y_rim(number, step, last, edges, rim):
+        for d in (0, 1):
+            for rows, lanes, value in pair(
+                face(number, d + 2), *SIDES[d + 2], step
+            ):
+                rim[d, 1 : last + 2, rows, lanes] = value
+        for k, (ox, oy) in enumerate(EDGES):
+            x = 0 if ox < 0 else last + 2
+            for rows, lanes, value in pair(lambda q: edges[k, q], ox, oy, step):
+                rim[0 if oy < 0 else 1, x, rows, lanes] = value[0]
+
+    def x_rim(number, step, last, rim):
+        for d in (0, 1):
+            for rows, lanes, value in pair(face(number, d), *SIDES[d], step):
+                rim[d, 1 : last + 2, rows, lanes] = value
 
     def centre_conv(z, wp, i):
         planes = [(1, i - 1), (0, i), (1, i), (0, i + 1)]
@@ -381,8 +393,8 @@
 
     def add_x(number, described, wp, finish):
         arrive(described, SIDES[:2])
-        received_sides((0, 1), 7, side_src, recv_side.at[number])
-        x_rim(1, side_src, zx, 8)
+        x_rim(number, 1, 7, zx)
+        edges_beside_x(number, edge_src)
         for d in (0, 1):
             i, h, p = (0, 0, 0) if d == 0 else (3, 1, 3)
             lhs = jnp.concatenate(
@@ -401,27 +413,21 @@
 
     def add_y(number, described, wp, finish):
         arrive(described, EDGES + SIDES[2:])
-        received_sides((2, 3), 7, side_src, recv_side.at[number])
-        received_edges(7, side_src, edge_src, recv_edge.at[number])
-        fine_y_rim()
+        edges_beside_y(number, edge_src, recv_edge.at[number])
+        y_rim(number, 1, 7, edge_src, zy)
         for d in (0, 1):
             y, ky = (0, 0) if d == 0 else (7, 2)
             lhs = jnp.concatenate(
-                [
-                    zy[d, p % 2, p // 2 : p // 2 + 4].reshape(128, 384)
-                    for p in range(4)
-                ],
-                axis=1,
+                [zy[d, kx : kx + 8].reshape(256, 384) for kx in range(3)], axis=1
             )
-            rhs = jnp.concatenate([wp[p, ky] for p in range(4)], axis=0)
+            rhs = jnp.concatenate([wp[kx, ky][:, 0:128] for kx in range(3)], axis=0)
             add = jnp.dot(lhs, rhs, preferred_element_type=F32)
-            for h in (0, 1):
-                part = add[:, 128 * h : 128 * h + 128].reshape(4, 32, 128)
-                part = (total[:, h, y] + part).reshape(4, 4, 8, 128)
-                for s in range(4):
-                    finish(s, (slice(0, 4), h, y), part[:, s])
-
-    own_sources(field, 7, side_src, edge_src)
+            part = total[:, :, y] + add.reshape(4, 2, 32, 128)
+            part = part.reshape(4, 2, 4, 8, 128)
+            for s in range(4):
+                finish(s, (slice(0, 4), slice(0, 2), y), part[:, :, s])
+
+    own_edges(field, 7, edge_src)
     fine_centre(field, zin)
 
     copies[4].wait()
@@ -436,11 +442,8 @@
     convolve(zin, w1p, to_hidden)
     add_x(0, sent, w1p, to_hidden)
     add_y(0, sent, w1p, to_hidden)
-    sent_hidden = exchange(
-        1, hidden, 7, send_side.at[1], send_edge.at[1], recv_side.at[1], recv_edge.at[1]
-    )
-    start(sent_hidden)
-    own_sources(hidden, 7, side_src, edge_src)
+    sent_hidden = exchange(1, hidden, 7, send_edge.at[1], recv_edge.at[1])
+    own_edges(hidden, 7, edge_src)
     fine_centre(hidden, zhid)
 
     for k in (6, 7, 8):
@@ -467,12 +470,9 @@
     pool((1, 2))
     add_y(1, sent_hidden, w2p, to_fine)
     pool((0, 3))
-    sent_coarse = exchange(
-        2, coarse_field, 3, csend_side, csend_edge, crecv_side, crecv_edge
-    )
-    start(sent_coarse)
-
-    own_sources(coarse_field, 3, cside_src, cedge_src)
+    sent_coarse = exchange(2, coarse_field, 3, csend_edge, crecv_edge)
+
+    own_edges(coarse_field, 3, cedge_src)
     for x in range(4):
         for rows, lanes, value in pair(lambda q: coarse_field[q, x], 0, 0, 2):
             zc[x + 1, 1:5, rows, lanes] = value
@@ -508,8 +508,8 @@
                         out[at] = (out[at] + raised) * live[s]
 
     arrive(sent_coarse, SIDES[:2])
-    received_sides((0, 1), 3, cside_src, crecv_side)
-    x_rim(2, cside_src, zcx, 4)
+    x_rim(2, 2, 3, zcx)
+    edges_beside_x(2, cedge_src)
     for d in (0, 1):
         lhs = jnp.concatenate(
             [zcx[d, ky : ky + 4].reshape(128, 384) for ky in range(3)], axis=1
@@ -519,16 +519,8 @@
         ctotal[3 * d] = ctotal[3 * d] + add.reshape(4, 32, 256)
     join((1, 2))
     arrive(sent_coarse, EDGES + SIDES[2:])
-    received_sides((2, 3), 3, cside_src, crecv_side)
-    received_edges(3, cside_src, cedge_src, crecv_edge)
-    for d in (0, 1):
-        for rows, lanes, value in pair(
-            lambda q: cside_src[d + 2, q], *SIDES[d + 2], 2
-        ):
-            zcy[d, 1:5, rows, lanes] = value
-    for k, (ox, oy) in enumerate(EDGES):
-        for rows, lanes, value in pair(lambda q: cedge_src[k, q], ox, oy, 2):
-            zcy[0 if oy < 0 else 1, 0 if ox < 0 else 5, rows, lanes] = value[0]
+    edges_beside_y(2, cedge_src, crecv_edge)
+    y_rim(2, 2, 3, cedge_src, zcy)
     for d in (0, 1):
         lhs = jnp.concatenate(
             [zcy[d, kx : kx + 4].reshape(128, 384) for kx in range(3)], axis=1
@@ -580,14 +572,12 @@
             pltpu.VMEM((5, 4, 2, 8, 8, 128), F32),
             pltpu.VMEM((5, 4, 2, 8, 8, 128), F32),
             pltpu.VMEM((5, 4, 4, 8, 128), F32),
-            pltpu.VMEM((4, 9, 8, 8, 128), F32),
             pltpu.VMEM((4, 17, 1, 8, 128), F32),
-            pltpu.VMEM((4, 9, 4, 8, 128), F32),
             pltpu.VMEM((4, 17, 1, 8, 128), F32),
             pltpu.VMEM((2, 4, 10, 32, 384), BF16),
             pltpu.VMEM((2, 4, 10, 32, 384), BF16),
             pltpu.VMEM((2, 10, 32, 384), BF16),
-            pltpu.VMEM((2, 2, 5, 32, 384), BF16),
+            pltpu.VMEM((2, 10, 32, 384), BF16),
             pltpu.VMEM((6, 6, 32, 384), BF16),
             pltpu.VMEM((2, 6, 32, 384), BF16),
             pltpu.VMEM((2, 6, 32, 384), BF16),
@@ -597,19 +587,17 @@
             pltpu.VMEM((256, 128), BF16),
             pltpu.VMEM((4, 2, 8, 32, 128), F32),
             pltpu.VMEM((4, 4, 32, 256), F32),
-            pltpu.VMEM((2, 4, 4, 64, 128), BF16),
             pltpu.VMEM((2, 4, 32, 128), BF16),
-            pltpu.VMEM((2, 4, 4, 64, 128), BF16),
             pltpu.VMEM((2, 4, 32, 128), BF16),
-            pltpu.VMEM((4, 4, 32, 128), BF16),
             pltpu.VMEM((4, 32, 128), BF16),
-            pltpu.VMEM((4, 4, 32, 128), BF16),
             pltpu.VMEM((4, 32, 128), BF16),
             pltpu.SemaphoreType.DMA((12,)),
             pltpu.SemaphoreType.DMA((2,)),
             pltpu.SemaphoreType.DMA((3, 8)),
             pltpu.SemaphoreType.DMA((3, 8)),
-        ],
+        ]
+        + [pltpu.VMEM((9, 64, 128), BF16)] * 8
+        + [pltpu.VMEM((9, 32, 128), BF16)] * 4,
         compiler_params=pltpu.CompilerParams(
             collective_id=0, has_side_effects=True, vmem_limit_bytes=48 * 2**20
         ),

time: 21.5 us -> 21.3 us (level)
  no operation moved by 1% of the time
where the time goes in v5:
time: 21.3 us; the launch traced here: 21 us
  Pallas kernels  20 us (94%)
  local copies, waits for them, and re-layouts  0.97 us (5%)
    pallas_call x1, Pallas kernels, local(): pl.pallas_call(functools.partial(kernel, gx, gy), out_shape=jax.ShapeDtyp...  20 us
    unnamed x1, local copies, waits for them, and re-layouts  0.97 us

profile of v5, /device:TPU:57, one launch (start us, length us, event | category | flops | bytes accessed | tf_op | source)
XLA Modules:
  0.0 21.0 jit_solution(5230466067482654109)
XLA Ops:
  0.0 20.0 %unet_window.1 = f32[4,4,2,8,8,128]{5,4,3,2,1,0:T(8,128)S(1)} custom-call(s32[4]{0:T(128)} %bitcast.17, s32[4,26]{1,0:T(4,128)} %bitcast.15, bf16[4,8,64,128]{3,2,1,0:T(8,128)(2,1)} %bitcast.14, bf16[3,3,384,128]{3,2,1,0:T(8,128)(2,1)} %bitcast.12, f32[1,128]{1,0:T(1,128)} %bitcast.18, bf16[3,3,384,128]{3,2,1,0:T(8,128)(2,1)} %bitcast.13, ...), custom_call_target="tpu_custom_call" | custom-call | flops 8000000000 | bytes 8000000 | tf_op jit(solution)/shard_map/unet_window/pallas_call | solution.py:559
  20.0 1.0 %copy.12 = f32[1,1,4,512,128]{4,3,2,1,0:T(8,128)} copy(f32[1,1,4,512,128]{4,3,2,1,0:T(8,128)S(1)} %bitcast.10) | data formatting | bytes 2097152

commit v6 on v5

--- a/solution.py
+++ b/solution.py
@@ -23,6 +23,10 @@
 EDGES = [(-1, -1), (-1, 1), (1, -1), (1, 1)]
 ALL = SIDES + EDGES
 FARTHEST = (4, 5, 6, 7, 2, 3, 0, 1)
+
+
+def edges_on(oy):
+    return [(k, edge) for k, edge in enumerate(EDGES) if edge[1] == oy]
 
 
 def edge_of(step, last):
@@ -193,8 +197,8 @@
                 face = across(source, s, edge_of(oy, last))
             sides[number][d][s] = face.reshape(8 * (last + 1), 128).astype(BF16)
 
-    def pack_edges(source, last, edges):
-        for d, (ox, oy) in enumerate(EDGES):
+    def pack_edges(source, last, edges, oy):
+        for d, (ox, oy) in edges_on(oy):
             edges[d] = jnp.concatenate(
                 [
                     column(source, s, edge_of(ox, last), edge_of(oy, last))
@@ -228,23 +232,24 @@
         for ox, oy in directions:
             when_inside(-ox, -oy, described[ox, oy].start)
 
-    def exchange(number, source, last, edges, redges):
-        described = describe(number, edges, redges)
-        pack_edges(source, last, edges)
-        for d in (2, 3):
-            pack_side(number, source, last, d)
-        start(described, EDGES + SIDES[2:])
+    def leave_y(number, described, source, last, edges, d):
+        oy = 1 - 2 * d
+        pack_edges(source, last, edges, oy)
+        pack_side(number, source, last, 3 - d)
+        start(described, [edge for _, edge in edges_on(oy)] + [(0, oy)])
+
+    def leave_x(number, described, source, last):
         for d in (0, 1):
             pack_side(number, source, last, d)
         start(described, SIDES[:2])
-        return described
 
     def arrive(described, directions):
         for ox, oy in directions:
             when_inside(ox, oy, described[ox, oy].wait_recv)
 
     sent = describe(0, send_edge.at[0], recv_edge.at[0])
-    pack_edges(field, 7, send_edge.at[0])
+    for oy in (-1, 1):
+        pack_edges(field, 7, send_edge.at[0], oy)
     for d in (2, 3):
         pack_side(0, field, 7, d)
     pl.semaphore_wait(barrier, partners)
@@ -343,23 +348,36 @@
             for s in range(4):
                 edges[k, 4 + s, 0] = end_of(number, SIDES.index((ox, 0)), s, oy)
 
-    def edges_beside_y(number, edges, redges):
-        for k, (ox, oy) in enumerate(EDGES):
+    def edges_beside_y(number, edges, redges, d):
+        for k, (ox, oy) in edges_on(2 * d - 1):
             far = redges[k].astype(F32)
             for s in range(4):
-                edges[k, 8 + s, 0] = end_of(number, SIDES.index((0, oy)), s, ox)
+                edges[k, 8 + s, 0] = end_of(number, d + 2, s, ox)
                 edges[k, 12 + s, 0] = far[8 * s : 8 * s + 8]
 
-    def y_rim(number, step, last, edges, rim):
-        for d in (0, 1):
-            for rows, lanes, value in pair(
-                face(number, d + 2), *SIDES[d + 2], step
-            ):
-                rim[d, 1 : last + 2, rows, lanes] = value
-        for k, (ox, oy) in enumerate(EDGES):
+    def y_rim(number, step, last, edges, rim, d):
+        for rows, lanes, value in pair(face(number, d + 2), *SIDES[d + 2], step):
+            rim[d, 1 : last + 2, rows, lanes] = value
+        for k, (ox, oy) in edges_on(2 * d - 1):
             x = 0 if ox < 0 else last + 2
             for rows, lanes, value in pair(lambda q: edges[k, q], ox, oy, step):
-                rim[0 if oy < 0 else 1, x, rows, lanes] = value[0]
+                rim[d, x, rows, lanes] = value[0]
+
+    def arrive_y(described, d):
+        arrive(described, [edge for _, edge in edges_on(2 * d - 1)] + [SIDES[d + 2]])
+
+    def by_turns(step):
+        far_low = lax.rem(my, 4) == 0
+
+        @pl.when(far_low)
+        def _():
+            step(1)
+
+        step(0)
+
+        @pl.when(jnp.logical_not(far_low))
+        def _():
+            step(1)
 
     def x_rim(number, step, last, rim):
         for d in (0, 1):
@@ -411,11 +429,11 @@
             for s in range(4):
                 finish(s, (i, h, slice(1, 7)), inner[:, s])
 
-    def add_y(number, described, wp, finish):
-        arrive(described, EDGES + SIDES[2:])
-        edges_beside_y(number, edge_src, recv_edge.at[number])
-        y_rim(number, 1, 7, edge_src, zy)
-        for d in (0, 1):
+    def add_y(number, described, wp, finish, after):
+        def step(d):
+            arrive_y(described, d)
+            edges_beside_y(number, edge_src, recv_edge.at[number], d)
+            y_rim(number, 1, 7, edge_src, zy, d)
             y, ky = (0, 0) if d == 0 else (7, 2)
             lhs = jnp.concatenate(
                 [zy[d, kx : kx + 8].reshape(256, 384) for kx in range(3)], axis=1
@@ -426,6 +444,9 @@
             part = part.reshape(4, 2, 4, 8, 128)
             for s in range(4):
                 finish(s, (slice(0, 4), slice(0, 2), y), part[:, :, s])
+            after(d)
+
+        by_turns(step)
 
     own_edges(field, 7, edge_src)
     fine_centre(field, zin)
@@ -441,8 +462,15 @@
 
     convolve(zin, w1p, to_hidden)
     add_x(0, sent, w1p, to_hidden)
-    add_y(0, sent, w1p, to_hidden)
-    sent_hidden = exchange(1, hidden, 7, send_edge.at[1], recv_edge.at[1])
+    sent_hidden = describe(1, send_edge.at[1], recv_edge.at[1])
+    add_y(
+        0,
+        sent,
+        w1p,
+        to_hidden,
+        lambda d: leave_y(1, sent_hidden, hidden, 7, send_edge.at[1], d),
+    )
+    leave_x(1, sent_hidden, hidden, 7)
     own_edges(hidden, 7, edge_src)
     fine_centre(hidden, zhid)
 
@@ -468,9 +496,14 @@
     convolve(zhid, w2p, to_fine)
     add_x(1, sent_hidden, w2p, to_fine)
     pool((1, 2))
-    add_y(1, sent_hidden, w2p, to_fine)
-    pool((0, 3))
-    sent_coarse = exchange(2, coarse_field, 3, csend_edge, crecv_edge)
+    sent_coarse = describe(2, csend_edge, crecv_edge)
+
+    def to_coarse(d):
+        pool((3 * d,))
+        leave_y(2, sent_coarse, coarse_field, 3, csend_edge, d)
+
+    add_y(1, sent_hidden, w2p, to_fine, to_coarse)
+    leave_x(2, sent_coarse, coarse_field, 3)
 
     own_edges(coarse_field, 3, cedge_src)
     for x in range(4):
@@ -518,10 +551,11 @@
         add = jnp.dot(lhs, rhs, preferred_element_type=F32)
         ctotal[3 * d] = ctotal[3 * d] + add.reshape(4, 32, 256)
     join((1, 2))
-    arrive(sent_coarse, EDGES + SIDES[2:])
-    edges_beside_y(2, cedge_src, crecv_edge)
-    y_rim(2, 2, 3, cedge_src, zcy)
-    for d in (0, 1):
+
+    def coarse_y(d):
+        arrive_y(sent_coarse, d)
+        edges_beside_y(2, cedge_src, crecv_edge, d)
+        y_rim(2, 2, 3, cedge_src, zcy, d)
         lhs = jnp.concatenate(
             [zcy[d, kx : kx + 4].reshape(128, 384) for kx in range(3)], axis=1
         )
@@ -534,7 +568,9 @@
         )
         add = jnp.dot(lhs, rhs, preferred_element_type=F32)
         ctotal[:, 3 * d] = ctotal[:, 3 * d] + add.reshape(4, 32, 256)
-    join((0, 3))
+        join((3 * d,))
+
+    by_turns(coarse_y)
     for described in (sent, sent_hidden, sent_coarse):
         for (ox, oy), copy in described.items():
             when_inside(-ox, -oy, copy.wait_send)

time: 21.3 us -> 21 us (0.986)
  Pallas kernels: 20 us -> 19.7 us
    pallas_call x1, Pallas kernels: 20 us -> 19.7 us  [local(): pl.pallas_call(functools.partial(kernel, gx, gy), out_shape=jax.ShapeDtyp...]
where the time goes in v6:
time: 21 us; the launch traced here: 20.7 us
  Pallas kernels  19.7 us (94%)
  local copies, waits for them, and re-layouts  0.97 us (5%)
    pallas_call x1, Pallas kernels, local(): pl.pallas_call(functools.partial(kernel, gx, gy), out_shape=jax.ShapeDtyp...  19.7 us
    unnamed x1, local copies, waits for them, and re-layouts  0.97 us

profile of v6, /device:TPU:57, one launch (start us, length us, event | category | flops | bytes accessed | tf_op | source)
XLA Modules:
  0.0 20.7 jit_solution(17843674822472874746)
XLA Ops:
  0.0 19.7 %unet_window.1 = f32[4,4,2,8,8,128]{5,4,3,2,1,0:T(8,128)S(1)} custom-call(s32[4]{0:T(128)} %bitcast.17, s32[4,26]{1,0:T(4,128)} %bitcast.15, bf16[4,8,64,128]{3,2,1,0:T(8,128)(2,1)} %bitcast.14, bf16[3,3,384,128]{3,2,1,0:T(8,128)(2,1)} %bitcast.12, f32[1,128]{1,0:T(1,128)} %bitcast.18, bf16[3,3,384,128]{3,2,1,0:T(8,128)(2,1)} %bitcast.13, ...), custom_call_target="tpu_custom_call" | custom-call | flops 8000000000 | bytes 8000000 | tf_op jit(solution)/shard_map/unet_window/pallas_call | solution.py:595
  19.7 1.0 %copy.12 = f32[1,1,4,512,128]{4,3,2,1,0:T(8,128)} copy(f32[1,1,4,512,128]{4,3,2,1,0:T(8,128)S(1)} %bitcast.10) | data formatting | bytes 2097152

commit v7 on v6

--- a/solution.py
+++ b/solution.py
@@ -234,9 +234,10 @@
 
     def leave_y(number, described, source, last, edges, d):
         oy = 1 - 2 * d
+        pack_side(number, source, last, 3 - d)
+        start(described, [(0, oy)])
         pack_edges(source, last, edges, oy)
-        pack_side(number, source, last, 3 - d)
-        start(described, [edge for _, edge in edges_on(oy)] + [(0, oy)])
+        start(described, [edge for _, edge in edges_on(oy)])
 
     def leave_x(number, described, source, last):
         for d in (0, 1):
@@ -252,8 +253,6 @@
         pack_edges(field, 7, send_edge.at[0], oy)
     for d in (2, 3):
         pack_side(0, field, 7, d)
-    pl.semaphore_wait(barrier, partners)
-    start(sent, EDGES + SIDES[2:] + SIDES[:2])
     copies[0].wait()
     for s in range(4):
         for x in range(8):
@@ -450,6 +449,8 @@
 
     own_edges(field, 7, edge_src)
     fine_centre(field, zin)
+    pl.semaphore_wait(barrier, partners)
+    start(sent, EDGES + SIDES[2:] + SIDES[:2])
 
     copies[4].wait()
     copies[5].wait()

time: 21 us -> 21.4 us (1.019)
  Pallas kernels: 19.7 us -> 20.2 us
    pallas_call x1, Pallas kernels: 19.7 us -> 20.2 us  [local(): pl.pallas_call(functools.partial(kernel, gx, gy), out_shape=jax.ShapeDtyp...]
where the time goes in v7:
time: 21.4 us; the launch traced here: 21.2 us
  Pallas kernels  20.2 us (94%)
  local copies, waits for them, and re-layouts  0.97 us (5%)
    pallas_call x1, Pallas kernels, local(): pl.pallas_call(functools.partial(kernel, gx, gy), out_shape=jax.ShapeDtyp...  20.2 us
    unnamed x1, local copies, waits for them, and re-layouts  0.97 us

profile of v7, /device:TPU:57, one launch (start us, length us, event | category | flops | bytes accessed | tf_op | source)
XLA Modules:
  0.0 21.2 jit_solution(9616550443530535252)
XLA Ops:
  0.0 20.2 %unet_window.1 = f32[4,4,2,8,8,128]{5,4,3,2,1,0:T(8,128)S(1)} custom-call(s32[4]{0:T(128)} %bitcast.17, s32[4,26]{1,0:T(4,128)} %bitcast.15, bf16[4,8,64,128]{3,2,1,0:T(8,128)(2,1)} %bitcast.14, bf16[3,3,384,128]{3,2,1,0:T(8,128)(2,1)} %bitcast.12, f32[1,128]{1,0:T(1,128)} %bitcast.18, bf16[3,3,384,128]{3,2,1,0:T(8,128)(2,1)} %bitcast.13, ...), custom_call_target="tpu_custom_call" | custom-call | flops 8000000000 | bytes 8000000 | tf_op jit(solution)/shard_map/unet_window/pallas_call | solution.py:596
  20.2 1.0 %copy.12 = f32[1,1,4,512,128]{4,3,2,1,0:T(8,128)} copy(f32[1,1,4,512,128]{4,3,2,1,0:T(8,128)S(1)} %bitcast.10) | data formatting | bytes 2097152

commit v8 on v6

--- a/solution.py
+++ b/solution.py
@@ -141,28 +141,38 @@
     for copy in rims + copies[:6]:
         copy.start()
 
-    for wp in (w1p, w2p):
+    def clear_weights(wp):
         wp[3, :, :, 0:128] = jnp.zeros((3, 384, 128), BF16)
         wp[0, :, :, 128:256] = jnp.zeros((3, 384, 128), BF16)
-    field[4] = jnp.zeros((4, 2, 8, 8, 128), F32)
-    hidden[4] = jnp.zeros((4, 2, 8, 8, 128), F32)
-    coarse_field[4] = jnp.zeros((4, 4, 8, 128), F32)
-    for d in range(4):
-        for number, rows in ((0, 64), (1, 64), (2, 32)):
-            sides[number][d][8] = jnp.zeros((rows, 128), BF16)
-        edge_src[d, 16] = jnp.zeros((1, 8, 128), F32)
-        cedge_src[d, 16] = jnp.zeros((1, 8, 128), F32)
-    for z in (zin, zhid):
+
+    def clear_ends(z):
         z[:, :, 0] = jnp.zeros((2, 4, 32, 384), BF16)
         z[:, :, 9] = jnp.zeros((2, 4, 32, 384), BF16)
-    for side in range(2):
-        for end in (0, 9):
-            zx[side, end] = jnp.zeros((32, 384), BF16)
+
+    clear_weights(w1p)
+    clear_ends(zin)
+    field[4] = jnp.zeros((4, 2, 8, 8, 128), F32)
+    for d in range(4):
+        sides[0][d][8] = jnp.zeros((64, 128), BF16)
+        edge_src[d, 16] = jnp.zeros((1, 8, 128), F32)
+
+    def clear_later():
+        clear_weights(w2p)
+        clear_ends(zhid)
+        hidden[4] = jnp.zeros((4, 2, 8, 8, 128), F32)
+        coarse_field[4] = jnp.zeros((4, 4, 8, 128), F32)
+        for d in range(4):
+            for number, rows in ((1, 64), (2, 32)):
+                sides[number][d][8] = jnp.zeros((rows, 128), BF16)
+            cedge_src[d, 16] = jnp.zeros((1, 8, 128), F32)
+        for side in range(2):
+            for end in (0, 9):
+                zx[side, end] = jnp.zeros((32, 384), BF16)
+            for end in (0, 5):
+                zcx[side, end] = jnp.zeros((32, 384), BF16)
         for end in (0, 5):
-            zcx[side, end] = jnp.zeros((32, 384), BF16)
-    for end in (0, 5):
-        zc[end] = jnp.zeros((6, 32, 384), BF16)
-        zc[:, end] = jnp.zeros((6, 32, 384), BF16)
+            zc[end] = jnp.zeros((6, 32, 384), BF16)
+            zc[:, end] = jnp.zeros((6, 32, 384), BF16)
 
     for copy in rims:
         copy.wait()
@@ -287,12 +297,14 @@
         return jnp.where(entry < 0, 16, place)
 
     where = {
-        (s, ox, oy, oz): index(s, ox, oy, oz)
-        for s in range(4)
-        for ox in (-1, 0, 1)
-        for oy in (-1, 0, 1)
-        for oz in (-1, 0, 1)
+        (s, 0, 0, oz): index(s, 0, 0, oz) for s in range(4) for oz in (-1, 0, 1)
     }
+
+    def index_rims():
+        for s in range(4):
+            for ox, oy in ALL:
+                for oz in (-1, 0, 1):
+                    where[s, ox, oy, oz] = index(s, ox, oy, oz)
 
     def shifted(low, own, high, step):
         row = lax.broadcasted_iota(jnp.int32, own.shape, own.ndim - 2)
@@ -314,13 +326,10 @@
                 ), both.astype(BF16)
 
     def fine_centre(source, z):
-        def body(m, carry):
+        for m in range(4):
             for h in (0, 1):
                 for rows, lanes, value in pair(lambda q: source[q, m, h], 0, 0, 1):
                     z[h, m, 1:9, rows, lanes] = value
-            return carry
-
-        lax.fori_loop(0, 4, body, 0)
 
     def face(number, d):
         def fetch(q):
@@ -448,13 +457,14 @@
 
         by_turns(step)
 
-    own_edges(field, 7, edge_src)
-    fine_centre(field, zin)
-
     copies[4].wait()
     copies[5].wait()
     for copy in copies[6:]:
         copy.start()
+    fine_centre(field, zin)
+    own_edges(field, 7, edge_src)
+    index_rims()
+    clear_later()
 
     def to_hidden(s, at, value):
         value = jnp.maximum(value + b1[...].reshape(1, 1, 128), 0.0) * live[s]
@@ -471,11 +481,10 @@
         lambda d: leave_y(1, sent_hidden, hidden, 7, send_edge.at[1], d),
     )
     leave_x(1, sent_hidden, hidden, 7)
+    for k in (6, 7, 8):
+        copies[k].wait()
     own_edges(hidden, 7, edge_src)
     fine_centre(hidden, zhid)
-
-    for k in (6, 7, 8):
-        copies[k].wait()
 
     def to_fine(s, at, value):
         value = value + b2[...].reshape(1, 1, 128) + field[(s,) + at]

time: 21 us -> 20.9 us (level)
  no operation moved by 1% of the time
where the time goes in v8:
time: 20.9 us; the launch traced here: 20.7 us
  Pallas kernels  19.7 us (94%)
  local copies, waits for them, and re-layouts  0.97 us (5%)
    pallas_call x1, Pallas kernels, local(): pl.pallas_call(functools.partial(kernel, gx, gy), out_shape=jax.ShapeDtyp...  19.7 us
    unnamed x1, local copies, waits for them, and re-layouts  0.97 us

profile of v8, /device:TPU:57, one launch (start us, length us, event | category | flops | bytes accessed | tf_op | source)
XLA Modules:
  0.0 20.7 jit_solution(238920196839267870)
XLA Ops:
  0.0 19.7 %unet_window.1 = f32[4,4,2,8,8,128]{5,4,3,2,1,0:T(8,128)S(1)} custom-call(s32[4]{0:T(128)} %bitcast.17, s32[4,26]{1,0:T(4,128)} %bitcast.15, bf16[4,8,64,128]{3,2,1,0:T(8,128)(2,1)} %bitcast.14, bf16[3,3,384,128]{3,2,1,0:T(8,128)(2,1)} %bitcast.12, f32[1,128]{1,0:T(1,128)} %bitcast.18, bf16[3,3,384,128]{3,2,1,0:T(8,128)(2,1)} %bitcast.13, ...), custom_call_target="tpu_custom_call" | custom-call | flops 8000000000 | bytes 8000000 | tf_op jit(solution)/shard_map/unet_window/pallas_call | solution.py:604
  19.7 1.0 %copy.12 = f32[1,1,4,512,128]{4,3,2,1,0:T(8,128)} copy(f32[1,1,4,512,128]{4,3,2,1,0:T(8,128)S(1)} %bitcast.10) | data formatting | bytes 2097152

commit v9 on v8

--- a/solution.py
+++ b/solution.py
@@ -138,7 +138,7 @@
         )
         for d in (0, 1)
     ]
-    for copy in rims + copies[:6]:
+    for copy in rims + copies[:4]:
         copy.start()
 
     def clear_weights(wp):
@@ -176,6 +176,8 @@
 
     for copy in rims:
         copy.wait()
+    for copy in copies[4:6]:
+        copy.start()
 
     def plane(source, s, x):
         if source is coarse_field:
@@ -242,6 +244,10 @@
         for ox, oy in directions:
             when_inside(-ox, -oy, described[ox, oy].start)
 
+    def left(described):
+        for (ox, oy), copy in described.items():
+            when_inside(-ox, -oy, copy.wait_send)
+
     def leave_y(number, described, source, last, edges, d):
         oy = 1 - 2 * d
         pack_edges(source, last, edges, oy)
@@ -549,6 +555,9 @@
                         at = (s, slice(0, 4), h, 2 * y + f)
                         out[at] = (out[at] + raised) * live[s]
 
+    left(sent)
+    left(sent_hidden)
+
     arrive(sent_coarse, SIDES[:2])
     x_rim(2, 2, 3, zcx)
     edges_beside_x(2, cedge_src)
@@ -560,6 +569,7 @@
         add = jnp.dot(lhs, rhs, preferred_element_type=F32)
         ctotal[3 * d] = ctotal[3 * d] + add.reshape(4, 32, 256)
     join((1, 2))
+    left(sent_coarse)
 
     def coarse_y(d):
         arrive_y(sent_coarse, d)
@@ -580,9 +590,6 @@
         join((3 * d,))
 
     by_turns(coarse_y)
-    for described in (sent, sent_hidden, sent_coarse):
-        for (ox, oy), copy in described.items():
-            when_inside(-ox, -oy, copy.wait_send)
 
 
 def local(gx, gy, features, slot_cell, neighbours, w1, b1, w2, b2, wc, bc, wl):

time: 20.9 us -> 20.8 us (level)
  no operation moved by 1% of the time
where the time goes in v9:
time: 20.8 us; the launch traced here: 20.6 us
  Pallas kernels  19.6 us (94%)
  local copies, waits for them, and re-layouts  0.97 us (5%)
    pallas_call x1, Pallas kernels, local(): pl.pallas_call(functools.partial(kernel, gx, gy), out_shape=jax.ShapeDtyp...  19.6 us
    unnamed x1, local copies, waits for them, and re-layouts  0.97 us

profile of v9, /device:TPU:57, one launch (start us, length us, event | category | flops | bytes accessed | tf_op | source)
XLA Modules:
  0.0 20.6 jit_solution(7333577624924337996)
XLA Ops:
  0.0 19.6 %unet_window.1 = f32[4,4,2,8,8,128]{5,4,3,2,1,0:T(8,128)S(1)} custom-call(s32[4]{0:T(128)} %bitcast.17, s32[4,26]{1,0:T(4,128)} %bitcast.15, bf16[4,8,64,128]{3,2,1,0:T(8,128)(2,1)} %bitcast.14, bf16[3,3,384,128]{3,2,1,0:T(8,128)(2,1)} %bitcast.12, f32[1,128]{1,0:T(1,128)} %bitcast.18, bf16[3,3,384,128]{3,2,1,0:T(8,128)(2,1)} %bitcast.13, ...), custom_call_target="tpu_custom_call" | custom-call | flops 8000000000 | bytes 8000000 | tf_op jit(solution)/shard_map/unet_window/pallas_call | solution.py:611
  19.6 1.0 %copy.12 = f32[1,1,4,512,128]{4,3,2,1,0:T(8,128)} copy(f32[1,1,4,512,128]{4,3,2,1,0:T(8,128)S(1)} %bitcast.10) | data formatting | bytes 2097152

commit v10 on v9

--- a/solution.py
+++ b/solution.py
@@ -163,7 +163,9 @@
         coarse_field[4] = jnp.zeros((4, 4, 8, 128), F32)
         for d in range(4):
             for number, rows in ((1, 64), (2, 32)):
-                sides[number][d][8] = jnp.zeros((rows, 128), BF16)
+                sides[number][d][4 if number == 2 else 8] = jnp.zeros(
+                    (rows, 128), BF16
+                )
             cedge_src[d, 16] = jnp.zeros((1, 8, 128), F32)
         for side in range(2):
             for end in (0, 9):
@@ -202,12 +204,28 @@
 
     def pack_side(number, source, last, d):
         ox, oy = SIDES[d]
+        faces = []
         for s in range(4):
             if oy == 0:
-                face = plane(source, s, edge_of(ox, last))
+                faces.append(plane(source, s, edge_of(ox, last)))
             else:
-                face = across(source, s, edge_of(oy, last))
-            sides[number][d][s] = face.reshape(8 * (last + 1), 128).astype(BF16)
+                faces.append(across(source, s, edge_of(oy, last)))
+        if number == 2:
+            even = lax.broadcasted_iota(jnp.int32, faces[0].shape, 1) % 2 == 0
+            faces = [
+                jnp.where(even, faces[2 * k], faces[2 * k + 1]) for k in (0, 1)
+            ]
+        for k, value in enumerate(faces):
+            sides[number][d][k] = value.reshape(8 * (last + 1), 128).astype(BF16)
+
+    def doubled(value, parity):
+        axis = value.ndim - 2
+        row = lax.broadcasted_iota(jnp.int32, value.shape, axis) % 2
+        after = pltpu.roll(value, 1, axis)
+        before = pltpu.roll(value, 7, axis)
+        return jnp.where(
+            row == parity, value, jnp.where(row == 1, after, before)
+        )
 
     def pack_edges(source, last, edges, oy):
         for d, (ox, oy) in edges_on(oy):
@@ -224,8 +242,9 @@
         for k in FARTHEST:
             ox, oy = ALL[k]
             if k < 4:
-                src = sides[number][k].at[0:4]
-                dst = sides[number][k].at[4:8]
+                count = 2 if number == 2 else 4
+                src = sides[number][k].at[0:count]
+                dst = sides[number][k].at[count : 2 * count]
                 if number == 0 and oy == 0:
                     src = feat.at[:, edge_of(ox, 7)]
             else:
@@ -339,8 +358,10 @@
 
     def face(number, d):
         def fetch(q):
-            value = sides[number][d][q].astype(F32)
-            return value.reshape(value.shape[0] // 8, 8, 128)
+            if number == 2:
+                value = sides[2][d][lax.shift_right_logical(q, 1)].astype(F32)
+                return doubled(value.reshape(4, 8, 128), lax.bitwise_and(q, 1))
+            return sides[number][d][q].astype(F32).reshape(8, 8, 128)
 
         return fetch
 
@@ -353,10 +374,13 @@
 
     def end_of(number, d, s, step):
         ref = sides[number][d]
+        at = 2 + s // 2 if number == 2 else 4 + s
         if step < 0:
             rows = ref.shape[1]
-            return ref[4 + s, rows - 16 : rows].astype(F32)[8:16]
-        return ref[4 + s, 0:16].astype(F32)[0:8]
+            value = ref[at, rows - 16 : rows].astype(F32)[8:16]
+        else:
+            value = ref[at, 0:16].astype(F32)[0:8]
+        return doubled(value, s % 2) if number == 2 else value
 
     def edges_beside_x(number, edges):
         for k, (ox, oy) in enumerate(EDGES):
@@ -649,7 +673,7 @@
             pltpu.SemaphoreType.DMA((3, 8)),
         ]
         + [pltpu.VMEM((9, 64, 128), BF16)] * 8
-        + [pltpu.VMEM((9, 32, 128), BF16)] * 4,
+        + [pltpu.VMEM((5, 32, 128), BF16)] * 4,
         compiler_params=pltpu.CompilerParams(
             collective_id=0, has_side_effects=True, vmem_limit_bytes=48 * 2**20
         ),

time: 20.8 us -> 20.6 us (level)
  no operation moved by 1% of the time
where the time goes in v10:
time: 20.6 us; the launch traced here: 20.5 us
  Pallas kernels  19.5 us (95%)
  local copies, waits for them, and re-layouts  0.97 us (5%)
    pallas_call x1, Pallas kernels, local(): pl.pallas_call(functools.partial(kernel, gx, gy), out_shape=jax.ShapeDtyp...  19.5 us
    unnamed x1, local copies, waits for them, and re-layouts  0.97 us

profile of v10, /device:TPU:57, one launch (start us, length us, event | category | flops | bytes accessed | tf_op | source)
XLA Modules:
  0.0 20.5 jit_solution(18116134487064557026)
XLA Ops:
  0.0 19.5 %unet_window.1 = f32[4,4,2,8,8,128]{5,4,3,2,1,0:T(8,128)S(1)} custom-call(s32[4]{0:T(128)} %bitcast.17, s32[4,26]{1,0:T(4,128)} %bitcast.15, bf16[4,8,64,128]{3,2,1,0:T(8,128)(2,1)} %bitcast.14, bf16[3,3,384,128]{3,2,1,0:T(8,128)(2,1)} %bitcast.12, f32[1,128]{1,0:T(1,128)} %bitcast.18, bf16[3,3,384,128]{3,2,1,0:T(8,128)(2,1)} %bitcast.13, ...), custom_call_target="tpu_custom_call" | custom-call | flops 8000000000 | bytes 8000000 | tf_op jit(solution)/shard_map/unet_window/pallas_call | solution.py:635
  19.5 1.0 %copy.12 = f32[1,1,4,512,128]{4,3,2,1,0:T(8,128)} copy(f32[1,1,4,512,128]{4,3,2,1,0:T(8,128)S(1)} %bitcast.10) | data formatting | bytes 2097152

commit v11 on v10

--- a/solution.py
+++ b/solution.py
@@ -270,7 +270,8 @@
     def leave_y(number, described, source, last, edges, d):
         oy = 1 - 2 * d
         pack_edges(source, last, edges, oy)
-        pack_side(number, source, last, 3 - d)
+        if number == 2:
+            pack_side(number, source, last, 3 - d)
         start(described, [edge for _, edge in edges_on(oy)] + [(0, oy)])
 
     def leave_x(number, described, source, last):
@@ -498,7 +499,10 @@
 
     def to_hidden(s, at, value):
         value = jnp.maximum(value + b1[...].reshape(1, 1, 128), 0.0) * live[s]
-        hidden[(s,) + at] = value.astype(BF16).astype(F32)
+        value = value.astype(BF16)
+        if at[2] == 0 or at[2] == 7:
+            sides[1][3 if at[2] == 0 else 2][s] = value.reshape(64, 128)
+        hidden[(s,) + at] = value.astype(F32)
 
     convolve(zin, w1p, to_hidden)
     add_x(0, sent, w1p, to_hidden)

time: 20.6 us -> 20.6 us (level)
  no operation moved by 1% of the time
where the time goes in v11:
time: 20.6 us; the launch traced here: 20.5 us
  Pallas kernels  19.5 us (95%)
  local copies, waits for them, and re-layouts  0.97 us (5%)
    pallas_call x1, Pallas kernels, local(): pl.pallas_call(functools.partial(kernel, gx, gy), out_shape=jax.ShapeDtyp...  19.5 us
    unnamed x1, local copies, waits for them, and re-layouts  0.97 us

profile of v11, /device:TPU:57, one launch (start us, length us, event | category | flops | bytes accessed | tf_op | source)
XLA Modules:
  0.0 20.5 jit_solution(2270247465242276214)
XLA Ops:
  0.0 19.5 %unet_window.1 = f32[4,4,2,8,8,128]{5,4,3,2,1,0:T(8,128)S(1)} custom-call(s32[4]{0:T(128)} %bitcast.17, s32[4,26]{1,0:T(4,128)} %bitcast.15, bf16[4,8,64,128]{3,2,1,0:T(8,128)(2,1)} %bitcast.14, bf16[3,3,384,128]{3,2,1,0:T(8,128)(2,1)} %bitcast.12, f32[1,128]{1,0:T(1,128)} %bitcast.18, bf16[3,3,384,128]{3,2,1,0:T(8,128)(2,1)} %bitcast.13, ...), custom_call_target="tpu_custom_call" | custom-call | flops 8000000000 | bytes 8000000 | tf_op jit(solution)/shard_map/unet_window/pallas_call | solution.py:639
  19.5 1.0 %copy.12 = f32[1,1,4,512,128]{4,3,2,1,0:T(8,128)} copy(f32[1,1,4,512,128]{4,3,2,1,0:T(8,128)S(1)} %bitcast.10) | data formatting | bytes 2097152

commit v12 on v10

--- a/solution.py
+++ b/solution.py
@@ -387,12 +387,10 @@
             for s in range(4):
                 edges[k, 4 + s, 0] = end_of(number, SIDES.index((ox, 0)), s, oy)
 
-    def edges_beside_y(number, edges, redges, d):
+    def edges_beside_y(number, edges, d):
         for k, (ox, oy) in edges_on(2 * d - 1):
-            far = redges[k].astype(F32)
             for s in range(4):
                 edges[k, 8 + s, 0] = end_of(number, d + 2, s, ox)
-                edges[k, 12 + s, 0] = far[8 * s : 8 * s + 8]
 
     def y_rim(number, step, last, edges, rim, d):
         for rows, lanes, value in pair(face(number, d + 2), *SIDES[d + 2], step):
@@ -402,8 +400,13 @@
             for rows, lanes, value in pair(lambda q: edges[k, q], ox, oy, step):
                 rim[d, x, rows, lanes] = value[0]
 
-    def arrive_y(described, d):
-        arrive(described, [edge for _, edge in edges_on(2 * d - 1)] + [SIDES[d + 2]])
+    def arrive_y(described, d, edges, redges):
+        arrive(described, [edge for _, edge in edges_on(2 * d - 1)])
+        for k, _ in edges_on(2 * d - 1):
+            far = redges[k].astype(F32)
+            for s in range(4):
+                edges[k, 12 + s, 0] = far[8 * s : 8 * s + 8]
+        arrive(described, [SIDES[d + 2]])
 
     def by_turns(step):
         far_low = lax.rem(my, 4) == 0
@@ -470,8 +473,8 @@
 
     def add_y(number, described, wp, finish, after):
         def step(d):
-            arrive_y(described, d)
-            edges_beside_y(number, edge_src, recv_edge.at[number], d)
+            arrive_y(described, d, edge_src, recv_edge.at[number])
+            edges_beside_y(number, edge_src, d)
             y_rim(number, 1, 7, edge_src, zy, d)
             y, ky = (0, 0) if d == 0 else (7, 2)
             lhs = jnp.concatenate(
@@ -596,8 +599,8 @@
     left(sent_coarse)
 
     def coarse_y(d):
-        arrive_y(sent_coarse, d)
-        edges_beside_y(2, cedge_src, crecv_edge, d)
+        arrive_y(sent_coarse, d, cedge_src, crecv_edge)
+        edges_beside_y(2, cedge_src, d)
         y_rim(2, 2, 3, cedge_src, zcy, d)
         lhs = jnp.concatenate(
             [zcy[d, kx : kx + 4].reshape(128, 384) for kx in range(3)], axis=1

time: 20.6 us -> 20.6 us (level)
  no operation moved by 1% of the time
where the time goes in v12:
time: 20.6 us; the launch traced here: 20.5 us
  Pallas kernels  19.5 us (95%)
  local copies, waits for them, and re-layouts  0.97 us (5%)
    pallas_call x1, Pallas kernels, local(): pl.pallas_call(functools.partial(kernel, gx, gy), out_shape=jax.ShapeDtyp...  19.5 us
    unnamed x1, local copies, waits for them, and re-layouts  0.97 us

profile of v12, /device:TPU:57, one launch (start us, length us, event | category | flops | bytes accessed | tf_op | source)
XLA Modules:
  0.0 20.5 jit_solution(940394421717087192)
XLA Ops:
  0.0 19.5 %unet_window.1 = f32[4,4,2,8,8,128]{5,4,3,2,1,0:T(8,128)S(1)} custom-call(s32[4]{0:T(128)} %bitcast.17, s32[4,26]{1,0:T(4,128)} %bitcast.15, bf16[4,8,64,128]{3,2,1,0:T(8,128)(2,1)} %bitcast.14, bf16[3,3,384,128]{3,2,1,0:T(8,128)(2,1)} %bitcast.12, f32[1,128]{1,0:T(1,128)} %bitcast.18, bf16[3,3,384,128]{3,2,1,0:T(8,128)(2,1)} %bitcast.13, ...), custom_call_target="tpu_custom_call" | custom-call | flops 8000000000 | bytes 8000000 | tf_op jit(solution)/shard_map/unet_window/pallas_call | solution.py:638
  19.5 1.0 %copy.12 = f32[1,1,4,512,128]{4,3,2,1,0:T(8,128)} copy(f32[1,1,4,512,128]{4,3,2,1,0:T(8,128)S(1)} %bitcast.10) | data formatting | bytes 2097152
